TPU v7x, 32 devices: a whole 2x2x4 slice. The times are simulated.
32 devices in a mesh: strip: 4 (over y, x), along: 8 (over z, core).
Axes of the slice: x: 2, y: 2, z: 4, core: 2. Of those that a mesh axis runs over, the one named last changes fastest.
Arguments:
- images: float32 [256, 4096], P('strip', 'along'), may hold values from 0 to 255
- offsets: int32 [4, 8, 2], P('strip', 'along'), may hold values from 0 to 31
Outputs:
- matches: float32 [8, 256, 4096], P(None, 'strip', 'along')
All inputs are finite; a program needn't handle non-finite values.
Results may differ from a plain program's by a relative error of at most 0.000063.
Values sent between devices are 32-bit elements; how exact they have to be, the bound alone decides.
No kernel may reach another device: no remote copies, remote signals or barrier semaphores. Data moves between devices by JAX's collectives and lax.ppermute only.
A program may use at most 64 MiB of HBM per device.

v0:
```python
import functools
import math

import jax
import jax.numpy as jnp
from jax import lax
from jax.experimental import pallas as pl
from jax.experimental.pallas import tpu as pltpu
from jax.sharding import PartitionSpec as P

DISP = 16
RADIUS = 4
LANES, SUBS = 128, 8
GROUP = 4
CENTRE = 128.0
VMEM_LIMIT = 24 * 2**20
f32, bf16, i32 = jnp.float32, jnp.bfloat16, jnp.int32
IN_VMEM = pl.BlockSpec(memory_space=pltpu.VMEM)
IN_SMEM = pl.BlockSpec(memory_space=pltpu.SMEM)
IN_ANY = pl.BlockSpec(memory_space=pl.ANY)


def iota(axis):
    return lax.broadcasted_iota(i32, (SUBS, LANES), axis)


def loop(n, body, unroll=True):
    lax.fori_loop(0, n, lambda i, c: (body(i), c)[1], 0, unroll=unroll)


def swap(x, n):
    return jnp.take_along_axis(x, iota(1) ^ n, axis=1, mode="promise_in_bounds")


def sums(x):
    front = [x[0]]
    for i in range(1, 8):
        front.append(front[-1] + x[i])
    back = [front[7]] + [x[7]] * 7
    for i in range(6, 0, -1):
        back[i] = back[i + 1] + x[i]
    return front, back


def box_cols(x):
    lane = iota(1)
    fa, ba = sums(x[:8])
    fb, bb = sums(x[8:])
    before = lambda y: jnp.where(lane >= GROUP, pltpu.roll(y, GROUP, 1), 0.0)
    after = lambda y: jnp.where(lane < LANES - GROUP, pltpu.roll(y, LANES - GROUP, 1), 0.0)
    out = [before(bb[k + 4]) + fa[k + 4] for k in range(4)]
    out += [ba[k] + fb[k] for k in range(8)]
    return out + [bb[k] + after(fa[k]) for k in range(4)]


def box_rows(x):
    sub = iota(0)
    front, back = sums(x)
    before = lambda y: jnp.where(sub >= 1, pltpu.roll(y, 1, 0), 0.0)
    after = lambda y: jnp.where(sub < SUBS - 1, pltpu.roll(y, SUBS - 1, 0), 0.0)
    return [before(back[j + 4]) + front[j + 4] for j in range(4)] + [back[j] + after(front[j]) for j in range(4)]


def make_order(order_ref):
    width = order_ref.shape[0]
    nv = width // LANES
    row = lax.broadcasted_iota(i32, (width, LANES), 0)
    lane = lax.broadcasted_iota(i32, (width, LANES), 1)
    for v in range(nv):
        order_ref[:, v * LANES:(v + 1) * LANES] = jnp.where(row == nv * lane + v, 1.0, 0.0).astype(bf16)


def reorder(x, order_ref, back=False):
    rows = x.shape[0]
    hi = x.astype(bf16)
    rest = x - hi.astype(f32)
    mid = rest.astype(bf16)
    low = (rest - mid.astype(f32)).astype(bf16)
    dims = (((1,), (1 if back else 0,)), ((), ()))
    y = lax.dot_general(jnp.concatenate([hi, mid, low]), order_ref[...], dims, preferred_element_type=f32)
    return (y[:rows] + y[rows:2 * rows]) + y[2 * rows:]


def put(ref, x):
    for v in range(ref.shape[0]):
        ref[v] = x[:, v * LANES:(v + 1) * LANES]


def inverse_counts(inv_ref, height, width):
    lane, sub = iota(1), iota(0)
    kk = inv_ref.shape[1]
    count = lambda i, n: 1.0 / (jnp.minimum(i + RADIUS, n - 1) - jnp.maximum(i - RADIUS, 0) + 1).astype(f32)
    cols = [count(lane // GROUP * kk + k, width) for k in range(kk)]
    for j in range(8):
        row = count(sub * 8 + j, height)
        for k in range(kk):
            inv_ref[j, k] = row * cols[k]


def guide_stats(v_ref, stats, inv_ref, p_ref, q_ref):
    g_ref, a1_ref, a2_ref, mean_ref = stats
    nv, kk = v_ref.shape[0], inv_ref.shape[1]
    first_lane = iota(1) // GROUP * GROUP

    def spread(h):
        for j in range(8):
            for v in range(nv):
                x = v_ref[v, pl.ds(j, SUBS, stride=8)]
                g_ref[j, nv * h + v] = jnp.take_along_axis(x, first_lane + h, axis=1, mode="promise_in_bounds")
    loop(GROUP, spread, 1)

    def first(j):
        g = [g_ref[j, k] for k in range(kk)]
        for k, y in enumerate(box_cols(g)):
            p_ref[j, k] = y
        for k, y in enumerate(box_cols([x * x for x in g])):
            q_ref[j, k] = y
    loop(8, first)

    def second(k):
        s1 = box_rows([p_ref[j, k] for j in range(8)])
        s2 = box_rows([q_ref[j, k] for j in range(8)])
        for j in range(8):
            inv = inv_ref[j, k]
            mean = s1[j] * inv
            a1 = inv / (s2[j] * inv - mean * mean + 50.0)
            a1_ref[j, k] = a1
            a2_ref[j, k] = a1 * mean
            mean_ref[j, k] = mean
    loop(kk, second)


def forward_partner(v_ref, y_ref, t):
    nv = v_ref.shape[0]

    def body(m):
        n = m + t
        a = lax.rem(LANES - lax.rem(lax.div(n, nv), LANES), LANES)
        for j in range(8):
            y_ref[m, j] = pltpu.roll(v_ref[lax.rem(n, nv), pl.ds(j, SUBS, stride=8)], a, 1)
    loop(y_ref.shape[0], body)


def side_partner(v2_ref, z_ref, t):
    nv, height = v2_ref.shape[0], v2_ref.shape[1] // 2
    odd, upper = iota(1) % 2 == 1, iota(1) % GROUP >= 2

    def one(m):
        start = [lax.rem(m + t + GROUP * h, height) for h in range(GROUP)]
        for v in range(nv):
            x = [v2_ref[v, pl.ds(start[h], SUBS, stride=8)] for h in range(GROUP)]
            for n in (0, 2):
                z_ref[m, nv * n + v] = jnp.where(odd, swap(x[n + 1], 1), x[n])
                z_ref[m, nv * (n + 1) + v] = jnp.where(odd, x[n + 1], swap(x[n], 1))
    loop(z_ref.shape[0], one)

    def two(m):
        for v in range(nv):
            for n in (0, 1):
                x, y = z_ref[m, nv * n + v], z_ref[m, nv * (n + 2) + v]
                z_ref[m, nv * n + v] = jnp.where(upper, swap(y, 2), x)
                z_ref[m, nv * (n + 2) + v] = jnp.where(upper, y, swap(x, 2))
    loop(z_ref.shape[0], two)


def pair_maps(partner, stats, inv_ref, work, out_ref):
    g_ref, a1_ref, a2_ref, mean_ref = stats
    p_ref, q_ref, a_ref, b_ref, score_ref = work
    kk = g_ref.shape[1]
    levels = DISP // GROUP

    def level(d):
        def first(j):
            g = [g_ref[j, k] for k in range(kk)]
            cost = [jnp.abs(g[k] - partner(j, k, d)) for k in range(kk)]
            for k, y in enumerate(box_cols(cost)):
                p_ref[j, k] = y
            for k, y in enumerate(box_cols([x * y for x, y in zip(g, cost)])):
                q_ref[j, k] = y
        loop(8, first)

        def second(k):
            p = box_rows([p_ref[j, k] for j in range(8)])
            q = box_rows([q_ref[j, k] for j in range(8)])
            ca = [q[j] * a1_ref[j, k] - p[j] * a2_ref[j, k] for j in range(8)]
            cb = [p[j] * inv_ref[j, k] - ca[j] * mean_ref[j, k] for j in range(8)]
            for j, y in enumerate(box_rows(ca)):
                a_ref[j, k] = y
            for j, y in enumerate(box_rows(cb)):
                b_ref[j, k] = y
        loop(kk, second)

        def third(j):
            a = box_cols([a_ref[j, k] for k in range(kk)])
            b = box_cols([b_ref[j, k] for k in range(kk)])
            for k in range(kk):
                score_ref[d, j, k] = (a[k] * g_ref[j, k] + b[k]) * (inv_ref[j, k] * (-4.0 * math.log2(math.e)))
        loop(8, third)
    loop(levels, level, 1)

    nv = kk // GROUP
    odd, upper = iota(1) % 2 == 1, iota(1) % GROUP >= 2
    lane_level = (iota(1) % GROUP * levels).astype(f32)

    def tops(j):
        for k in range(kk):
            top = functools.reduce(jnp.maximum, [score_ref[d, j, k] for d in range(levels)])
            top = jnp.maximum(top, swap(top, 1))
            b_ref[j, k] = jnp.maximum(top, swap(top, 2))
    loop(8, tops)

    def weights(j):
        for k in range(kk):
            w = [jnp.exp2(score_ref[d, j, k] - b_ref[j, k]) for d in range(levels)]
            s = w[-1]
            t = s
            for d in range(levels - 2, 0, -1):
                s = s + w[d]
                t = t + s
            s = s + w[0]
            p_ref[j, k] = s
            q_ref[j, k] = t + lane_level * s
            a_ref[j, k] = functools.reduce(jnp.add, [x * x for x in w])
    loop(8, weights, 1)

    def halves(j):
        for v in range(nv):
            for ref in (p_ref, q_ref, a_ref):
                x = [ref[j, nv * h + v] for h in range(GROUP)]
                for n in (0, 2):
                    ref[j, n // 2 * nv + v] = jnp.where(odd, x[n + 1], x[n]) + swap(jnp.where(odd, x[n], x[n + 1]), 1)
    loop(8, halves)

    height = out_ref.shape[1] // 2

    def last(j):
        for v in range(nv):
            lo, hi = ([ref[j, n * nv + v] for ref in (p_ref, q_ref, a_ref)] for n in range(2))
            s, t, u = (jnp.where(upper, y, x) + swap(jnp.where(upper, x, y), 2) for x, y in zip(lo, hi))
            r = 1.0 / s
            out_ref[v, pl.ds(j, SUBS, stride=8)] = t * r
            out_ref[v, pl.ds(height + j, SUBS, stride=8)] = u * (r * r)
    loop(8, last)


def restore(out_ref, order_ref):
    return reorder(jnp.concatenate([out_ref[v] for v in range(out_ref.shape[0])], axis=1), order_ref, back=True)


def field(kk, *lead):
    return (*lead, 8, kk, SUBS, LANES)


def call(body, ins, in_specs, outs, out_specs, scratch, flops, name):
    return pl.pallas_call(
        body, in_specs=in_specs, out_specs=out_specs, out_shape=outs, scratch_shapes=scratch, name=name,
        compiler_params=pltpu.CompilerParams(vmem_limit_bytes=VMEM_LIMIT),
        cost_estimate=pl.CostEstimate(flops=flops, bytes_accessed=2**20, transcendentals=0),
    )(*ins)


def per_device(images, offsets):
    height, width = images.shape
    kk = width // LANES * GROUP
    nv = width // LANES
    assert height == 8 * SUBS and kk == DISP
    tile_field = jax.ShapeDtypeStruct(field(kk), f32)
    vmem = lambda *shape: pltpu.VMEM(shape, f32)
    work = [vmem(*field(kk))] * 4 + [vmem(*field(kk, DISP // GROUP))]
    base = offsets[0, 0]
    strip = lax.axis_index("strip")

    def shifted(value, axis, steps):
        n = lax.axis_size(axis)
        return lax.ppermute(value, axis, [(i, i + steps) for i in range(max(0, -steps), min(n, n - steps))])

    def pack(base_ref, image_ref, out_ref):
        out_ref[:height] = image_ref[...]
        out_ref[height:] = jnp.full((SUBS, width), base_ref[1].astype(f32))

    def prepare(image_ref, order_ref, v_ref, inv_ref, g_ref, a1_ref, a2_ref, mean_ref, p_ref, q_ref):
        make_order(order_ref)
        inverse_counts(inv_ref, height, width)
        put(v_ref, reorder(image_ref[...] - CENTRE, order_ref))
        guide_stats(v_ref, (g_ref, a1_ref, a2_ref, mean_ref), inv_ref, p_ref, q_ref)

    def forward(base_ref, other_ref, order_ref, inv_ref, g_ref, a1_ref, a2_ref, mean_ref, out_ref, *scratch):
        *work_refs, v_ref, y_ref, maps_ref = scratch
        put(v_ref, reorder(other_ref[...] - CENTRE, order_ref))
        forward_partner(v_ref, y_ref, base_ref[0])
        pair_maps(lambda j, k, d: y_ref[k + d, j], (g_ref, a1_ref, a2_ref, mean_ref), inv_ref, work_refs, maps_ref)
        maps = restore(maps_ref, order_ref)
        out_ref[0] = maps[:height]
        out_ref[1] = maps[height:]

    def side(base_ref, own_ref, back_ref, other_ref, order_ref, inv_ref, g_ref, a1_ref, a2_ref, mean_ref, first_ref, out_ref, *scratch):
        *work_refs, v2_ref, z_ref, maps_ref, res_ref, b0, b1, b2, b3, sems = scratch
        copies = [pltpu.make_async_copy(first_ref, out_ref.at[0:2], sems.at[0])]
        copies[0].start()
        partner = lambda j, k, d: z_ref[j + d, k]

        def send(n, row):
            copies.append(pltpu.make_async_copy(res_ref.at[n], out_ref.at[row:row + 2], sems.at[n + 1]))
            copies[-1].start()

        def finish(n):
            maps = restore(maps_ref, order_ref)
            res_ref[n, 0] = maps[:height]
            res_ref[n, 1] = maps[height:]

        def twice(x):
            put(v2_ref, jnp.concatenate([x, x]))

        twice(reorder(other_ref[...] - CENTRE, order_ref))
        side_partner(v2_ref, z_ref, base_ref[1])
        pair_maps(partner, (g_ref, a1_ref, a2_ref, mean_ref), inv_ref, work_refs, maps_ref)
        finish(0)
        send(0, 4)

        @pl.when(base_ref[2] > 0)
        def _():
            twice(reorder(back_ref[:height] - CENTRE, order_ref))
            guide_stats(v2_ref.at[:, :height], (b0, b1, b2, b3), inv_ref, work_refs[0], work_refs[1])
            for v in range(nv):
                v2_ref[v, :height] = own_ref[v]
                v2_ref[v, height:] = own_ref[v]
            t = jnp.max(back_ref[height:, :LANES]).astype(i32)
            side_partner(v2_ref, z_ref, t)
            pair_maps(partner, (b0, b1, b2, b3), inv_ref, work_refs, maps_ref)
            finish(1)

        @pl.when(base_ref[2] == 0)
        def _():
            res_ref[1] = jnp.zeros(res_ref.shape[1:], f32)

        send(1, 6)
        for copy in copies:
            copy.wait()

    fwd_image = shifted(images, "along", -1)
    side_image = shifted(images, "strip", -1)
    scalars = jnp.concatenate([base, strip.astype(i32)[None]])
    packed = call(
        pack, (scalars, images), [IN_SMEM, IN_VMEM],
        jax.ShapeDtypeStruct((height + SUBS, width), f32), IN_VMEM, [], 2**16, "pack",
    )
    back_image = shifted(packed, "strip", 1)
    order, own, inv, *stats = call(
        prepare, (images,), [IN_VMEM],
        [jax.ShapeDtypeStruct((width, width), bf16), jax.ShapeDtypeStruct((nv, height, LANES), f32)] + [tile_field] * 5,
        [IN_VMEM] * 7, [vmem(*field(kk))] * 2, 2**26, "prepare",
    )
    fwd_image, side_image, back_image = lax.optimization_barrier((fwd_image, side_image, back_image))
    maps_shape = vmem(nv, 2 * height, LANES)
    fwd_maps = call(
        forward, (scalars, fwd_image, order, inv, *stats), [IN_SMEM] + [IN_VMEM] * 7,
        jax.ShapeDtypeStruct((2, height, width), f32), IN_VMEM,
        work + [vmem(nv, height, LANES), vmem(kk + 3, 8, SUBS, LANES), maps_shape], 2**28, "forward",
    )
    fwd_back = shifted(fwd_maps, "along", 1)
    out = call(
        side, (scalars, own, back_image, side_image, order, inv, *stats, fwd_maps), [IN_SMEM] + [IN_VMEM] * 10,
        jax.ShapeDtypeStruct((8, height, width), f32), IN_ANY,
        work + [maps_shape, vmem(8 + 3, kk, SUBS, LANES), maps_shape, vmem(2, 2, height, width)]
        + [vmem(*field(kk))] * 4 + [pltpu.SemaphoreType.DMA((3,))], 2**29, "side",
    )
    return lax.dynamic_update_slice(out, fwd_back, (2, 0, 0))


def solution(mesh):
    return jax.shard_map(
        per_device, mesh=mesh, in_specs=(P("strip", "along"), P("strip", "along", None)),
        out_specs=P(None, "strip", "along"), check_vma=False,
    )
```

profile of v0, /device:TPU:19, one launch (start us, length us, event | category | flops | bytes accessed | tf_op | source)
XLA Modules:
  0.0 41.7 jit_solution(3833085072299562473)
XLA Ops:
  0.0 0.0 copy-start.1
  0.0 0.7 %copy-done.1 = s32[1,1,2]{2,1,0:T(1,128)S(1)} copy-done((s32[1,1,2]{2,1,0:T(1,128)S(1)}, s32[1,1,2]{2,1,0:T(1,128)}, u32[]{:S(2)}) %copy-start.1) | copy-done | bytes 32
  0.7 0.1 pad_add_fusion.base_ref
  0.7 0.0 copy-start
  0.7 0.9 %copy-done = f32[64,512]{1,0:T(8,128)S(1)} copy-done((f32[64,512]{1,0:T(8,128)S(1)}, f32[64,512]{1,0:T(8,128)}, u32[]{:S(2)}) %copy-start) | copy-done | bytes 131096
  1.6 0.5 %pack.1 = f32[72,512]{1,0:T(8,128)S(1)} custom-call(s32[3]{0:T(128)S(1)} %pad_add_fusion.base_ref, f32[64,512]{1,0:T(8,128)S(1)} %copy-done), custom_call_target="tpu_custom_call" | custom-call | flops 65536 | bytes 1048576 | tf_op jit(solution)/shard_map/pack/pallas_call | solution.py:255
  2.2 3.1 %collective-permute-start.2 = (f32[72,512]{1,0:T(8,128)S(1)}, f32[72,512]{1,0:T(8,128)S(1)}, u32[]{:S(2)}, u32[]{:S(2)}) collective-permute-start(f32[72,512]{1,0:T(8,128)S(1)} %pack.1), channel_id=1, source_target_pairs={{0,8},{8,16},{16,24},{1,9},{9,17},{17,25},{2,10},{10,18},{18,26},{... | collective-permute-start | bytes 442376 | tf_op jit(solution)/shard_map/ppermute | solution.py:275
  5.3 2.9 %collective-permute-start = (f32[64,512]{1,0:T(8,128)S(1)}, f32[64,512]{1,0:T(8,128)S(1)}, u32[]{:S(2)}, u32[]{:S(2)}) collective-permute-start(f32[64,512]{1,0:T(8,128)S(1)} %copy-done), channel_id=1, source_target_pairs={{1,0},{2,1},{3,2},{4,3},{5,4},{6,5},{7,6},{9,8},{10,9},{11,10},{12... | collective-permute-start | bytes 393224 | tf_op jit(solution)/shard_map/ppermute | solution.py:275
  8.2 2.2 %collective-permute-start.1 = (f32[64,512]{1,0:T(8,128)S(1)}, f32[64,512]{1,0:T(8,128)S(1)}, u32[]{:S(2)}, u32[]{:S(2)}) collective-permute-start(f32[64,512]{1,0:T(8,128)S(1)} %copy-done), channel_id=1, source_target_pairs={{8,0},{16,8},{24,16},{9,1},{17,9},{25,17},{10,2},{18,10},{26,18},{... | collective-permute-start | bytes 393224 | tf_op jit(solution)/shard_map/ppermute | solution.py:275
  10.4 1.4 %prepare.1 = (bf16[512,512]{1,0:T(8,128)(2,1)S(1)}, f32[4,64,128]{2,1,0:T(8,128)S(1)}, f32[8,16,8,128]{3,2,1,0:T(8,128)S(1)}, f32[8,16,8,128]{3,2,1,0:T(8,128)S(...) custom-call(f32[64,512]{1,0:T(8,128)S(1)} %copy-done), custom_call_target="tpu_custom_call" | custom-call | flops 67108864 | bytes 1048576 | tf_op jit(solution)/shard_map/prepare/pallas_call | solution.py:255
  11.7 0.3 collective-permute-done.other_ref
  12.0 4.1 %collective-permute-done.1.other_ref = f32[64,512]{1,0:T(8,128)S(1)} collective-permute-done((f32[64,512]{1,0:T(8,128)S(1)}, f32[64,512]{1,0:T(8,128)S(1)}, u32[]{:S(2)}, u32[]{:S(2)}) %collective-permute-start.1) | collective-permute-done | bytes 131104 | tf_op jit(solution)/shard_map/ppermute | solution.py:275
  16.1 0.0 collective-permute-done.2.back_ref
  16.1 6.5 %forward.1.first_ref = f32[2,64,512]{2,1,0:T(8,128)S(1)} custom-call(s32[3]{0:T(128)S(1)} %pad_add_fusion.base_ref, f32[64,512]{1,0:T(8,128)S(1)} %collective-permute-done.other_ref, bf16[512,512]{1,0:T(8,128)(2,1)S(1)} %get-tuple-element.18.order_ref, f32[8,16,8,128]{3,2,1,0:T(8,128)S(1)} %get-tuple-element.19.inv_ref, ...), custom_call_target="tpu_custom_call" | custom-call | flops 268435456 | bytes 1048576 | tf_op jit(solution)/shard_map/forward/pallas_call | solution.py:255
  22.6 3.9 %collective-permute-start.3 = (f32[2,64,512]{2,1,0:T(8,128)S(1)}, f32[2,64,512]{2,1,0:T(8,128)S(1)}, u32[]{:S(2)}, u32[]{:S(2)}) collective-permute-start(f32[2,64,512]{2,1,0:T(8,128)S(1)} %forward.1.first_ref), channel_id=1, source_target_pairs={{0,1},{1,2},{2,3},{3,4},{4,5},{5,6},{6,7},{8,9},{9,10},{10,11},{11... | collective-permute-start | bytes 786440 | tf_op jit(solution)/shard_map/ppermute | solution.py:275
  26.5 14.4 %side.1 = f32[8,64,512]{2,1,0:T(8,128)} custom-call(s32[3]{0:T(128)S(1)} %pad_add_fusion.base_ref, f32[4,64,128]{2,1,0:T(8,128)S(1)} %get-tuple-element.15.own_ref, f32[72,512]{1,0:T(8,128)S(1)} %collective-permute-done.2.back_ref, f32[64,512]{1,0:T(8,128)S(1)} %collective-permute-done.1.other_ref, bf16[512,512]{1,0:T(8,128)(2,1)S(1)} %get-tuple-element.18.order_ref, ...), custom_call_target="tpu_custom_call" | custom-call | flops 536870912 | bytes 1048576 | tf_op jit(solution)/shard_map/side/pallas_call | solution.py:255
  40.9 0.0 collective-permute-done.3
  41.0 0.7 %constant_dynamic-update-slice_fusion = f32[8,64,512]{2,1,0:T(8,128)} fusion(f32[8,64,512]{2,1,0:T(8,128)} %side.1, f32[2,64,512]{2,1,0:T(8,128)S(1)} %collective-permute-done.3), kind=kLoop, calls=%fused_computation.1 | loop fusion | bytes 524288 | tf_op jit(solution)/shard_map/dynamic_update_slice | solution.py:367
Async XLA Ops:
  0.0 0.7 %copy-start.1 = (s32[1,1,2]{2,1,0:T(1,128)S(1)}, s32[1,1,2]{2,1,0:T(1,128)}, u32[]{:S(2)}) copy-start(s32[1,1,2]{2,1,0:T(1,128)} %param.3) | copy-start | bytes 28
  0.7 0.9 %copy-start = (f32[64,512]{1,0:T(8,128)S(1)}, f32[64,512]{1,0:T(8,128)}, u32[]{:S(2)}) copy-start(f32[64,512]{1,0:T(8,128)} %image_ref.3) | copy-start | bytes 393220
  2.2 13.9 %collective-permute-start.2 = (f32[72,512]{1,0:T(8,128)S(1)}, f32[72,512]{1,0:T(8,128)S(1)}, u32[]{:S(2)}, u32[]{:S(2)}) collective-permute-start(f32[72,512]{1,0:T(8,128)S(1)} %pack.1), channel_id=1, source_target_pairs={{0,8},{8,16},{16,24},{1,9},{9,17},{17,25},{2,10},{10,18},{18,26},{... | collective-permute-start | bytes 442376 | tf_op jit(solution)/shard_map/ppermute | solution.py:275
  5.3 6.7 %collective-permute-start = (f32[64,512]{1,0:T(8,128)S(1)}, f32[64,512]{1,0:T(8,128)S(1)}, u32[]{:S(2)}, u32[]{:S(2)}) collective-permute-start(f32[64,512]{1,0:T(8,128)S(1)} %copy-done), channel_id=1, source_target_pairs={{1,0},{2,1},{3,2},{4,3},{5,4},{6,5},{7,6},{9,8},{10,9},{11,10},{12... | collective-permute-start | bytes 393224 | tf_op jit(solution)/shard_map/ppermute | solution.py:275
  8.2 7.9 %collective-permute-start.1 = (f32[64,512]{1,0:T(8,128)S(1)}, f32[64,512]{1,0:T(8,128)S(1)}, u32[]{:S(2)}, u32[]{:S(2)}) collective-permute-start(f32[64,512]{1,0:T(8,128)S(1)} %copy-done), channel_id=1, source_target_pairs={{8,0},{16,8},{24,16},{9,1},{17,9},{25,17},{10,2},{18,10},{26,18},{... | collective-permute-start | bytes 393224 | tf_op jit(solution)/shard_map/ppermute | solution.py:275
  22.6 18.3 %collective-permute-start.3 = (f32[2,64,512]{2,1,0:T(8,128)S(1)}, f32[2,64,512]{2,1,0:T(8,128)S(1)}, u32[]{:S(2)}, u32[]{:S(2)}) collective-permute-start(f32[2,64,512]{2,1,0:T(8,128)S(1)} %forward.1.first_ref), channel_id=1, source_target_pairs={{0,1},{1,2},{2,3},{3,4},{4,5},{5,6},{6,7},{8,9},{9,10},{10,11},{11... | collective-permute-start | bytes 786440 | tf_op jit(solution)/shard_map/ppermute | solution.py:275
where the time goes:
time: 41.9 us; the launch traced here: 41.7 us
  Pallas kernels  22.9 us (55%)
  starting transfers between devices  12 us (29%)
  waiting for transfers between devices  4.36 us (10%)
  local copies, waits for them, and re-layouts  2.28 us (5%)
    pallas_call x4, Pallas kernels, call(): pl.pallas_call(body, in_specs=in_specs, out_specs=out_specs, out_shape=ou...  22.9 us
    ppermute x4, starting transfers between devices, shifted(): lax.ppermute(value, axis, [(i, i + steps) for i in range(max(0, -steps),...  12 us
    ppermute x4, waiting for transfers between devices, shifted(): lax.ppermute(value, axis, [(i, i + steps) for i in range(max(0, -steps),...  4.36 us
    unnamed x4, local copies, waits for them, and re-layouts  1.56 us
  transfers between devices with their start and end apart: 4, of which 2 were waited for; matrix products, arithmetic and copies ran while one was open for 0% of the time, Pallas kernels for 38%

commit v1 on v0

--- a/solution.py
+++ b/solution.py
@@ -251,9 +251,10 @@
     return (*lead, 8, kk, SUBS, LANES)
 
 
-def call(body, ins, in_specs, outs, out_specs, scratch, flops, name):
+def call(body, ins, in_specs, outs, out_specs, scratch, flops, name, aliases={}):
     return pl.pallas_call(
         body, in_specs=in_specs, out_specs=out_specs, out_shape=outs, scratch_shapes=scratch, name=name,
+        input_output_aliases=aliases,
         compiler_params=pltpu.CompilerParams(vmem_limit_bytes=VMEM_LIMIT),
         cost_estimate=pl.CostEstimate(flops=flops, bytes_accessed=2**20, transcendentals=0),
     )(*ins)
@@ -267,104 +268,96 @@
     tile_field = jax.ShapeDtypeStruct(field(kk), f32)
     vmem = lambda *shape: pltpu.VMEM(shape, f32)
     work = [vmem(*field(kk))] * 4 + [vmem(*field(kk, DISP // GROUP))]
-    base = offsets[0, 0]
-    strip = lax.axis_index("strip")
 
     def shifted(value, axis, steps):
         n = lax.axis_size(axis)
         return lax.ppermute(value, axis, [(i, i + steps) for i in range(max(0, -steps), min(n, n - steps))])
 
-    def pack(base_ref, image_ref, out_ref):
-        out_ref[:height] = image_ref[...]
-        out_ref[height:] = jnp.full((SUBS, width), base_ref[1].astype(f32))
-
-    def prepare(image_ref, order_ref, v_ref, inv_ref, g_ref, a1_ref, a2_ref, mean_ref, p_ref, q_ref):
+    def prepare(base_ref, image_ref, order_ref, v_ref, packed_ref, inv_ref, g_ref, a1_ref, a2_ref, mean_ref, p_ref, q_ref):
+        packed_ref[:height] = image_ref[...]
+        packed_ref[height:] = jnp.full((SUBS, width), base_ref[0, 0, 0].astype(f32))
         make_order(order_ref)
         inverse_counts(inv_ref, height, width)
         put(v_ref, reorder(image_ref[...] - CENTRE, order_ref))
         guide_stats(v_ref, (g_ref, a1_ref, a2_ref, mean_ref), inv_ref, p_ref, q_ref)
 
-    def forward(base_ref, other_ref, order_ref, inv_ref, g_ref, a1_ref, a2_ref, mean_ref, out_ref, *scratch):
-        *work_refs, v_ref, y_ref, maps_ref = scratch
-        put(v_ref, reorder(other_ref[...] - CENTRE, order_ref))
-        forward_partner(v_ref, y_ref, base_ref[0])
-        pair_maps(lambda j, k, d: y_ref[k + d, j], (g_ref, a1_ref, a2_ref, mean_ref), inv_ref, work_refs, maps_ref)
+    def side(base_ref, other_ref, order_ref, inv_ref, g_ref, a1_ref, a2_ref, mean_ref, out_ref, *scratch):
+        *work_refs, v2_ref, z_ref, maps_ref = scratch
+        x = reorder(other_ref[...] - CENTRE, order_ref)
+        put(v2_ref, jnp.concatenate([x, x]))
+        side_partner(v2_ref, z_ref, base_ref[0, 0, 1])
+        pair_maps(lambda j, k, d: z_ref[j + d, k], (g_ref, a1_ref, a2_ref, mean_ref), inv_ref, work_refs, maps_ref)
         maps = restore(maps_ref, order_ref)
         out_ref[0] = maps[:height]
         out_ref[1] = maps[height:]
 
-    def side(base_ref, own_ref, back_ref, other_ref, order_ref, inv_ref, g_ref, a1_ref, a2_ref, mean_ref, first_ref, out_ref, *scratch):
-        *work_refs, v2_ref, z_ref, maps_ref, res_ref, b0, b1, b2, b3, sems = scratch
-        copies = [pltpu.make_async_copy(first_ref, out_ref.at[0:2], sems.at[0])]
-        copies[0].start()
-        partner = lambda j, k, d: z_ref[j + d, k]
-
-        def send(n, row):
-            copies.append(pltpu.make_async_copy(res_ref.at[n], out_ref.at[row:row + 2], sems.at[n + 1]))
-            copies[-1].start()
-
-        def finish(n):
-            maps = restore(maps_ref, order_ref)
-            res_ref[n, 0] = maps[:height]
-            res_ref[n, 1] = maps[height:]
-
-        def twice(x):
-            put(v2_ref, jnp.concatenate([x, x]))
-
-        twice(reorder(other_ref[...] - CENTRE, order_ref))
-        side_partner(v2_ref, z_ref, base_ref[1])
-        pair_maps(partner, (g_ref, a1_ref, a2_ref, mean_ref), inv_ref, work_refs, maps_ref)
-        finish(0)
-        send(0, 4)
-
-        @pl.when(base_ref[2] > 0)
+    def finish(maps_ref, order_ref, res_ref, out_ref, sem):
+        maps = restore(maps_ref, order_ref)
+        res_ref[0] = maps[:height]
+        res_ref[1] = maps[height:]
+        copy = pltpu.make_async_copy(res_ref, out_ref, sem)
+        copy.start()
+        return copy
+
+    def forward(base_ref, other_ref, order_ref, inv_ref, g_ref, a1_ref, a2_ref, mean_ref, side_ref, out_ref, *scratch):
+        *work_refs, v_ref, y_ref, maps_ref, res_ref, sems = scratch
+        copy = pltpu.make_async_copy(side_ref, out_ref.at[4:6], sems.at[0])
+        copy.start()
+        put(v_ref, reorder(other_ref[...] - CENTRE, order_ref))
+        forward_partner(v_ref, y_ref, base_ref[0, 0, 0])
+        pair_maps(lambda j, k, d: y_ref[k + d, j], (g_ref, a1_ref, a2_ref, mean_ref), inv_ref, work_refs, maps_ref)
+        finish(maps_ref, order_ref, res_ref, out_ref.at[0:2], sems.at[1]).wait()
+        copy.wait()
+
+    def backward(own_ref, back_ref, order_ref, inv_ref, side_ref, old_ref, out_ref, *scratch):
+        *work_refs, v_ref, y_ref, maps_ref, res_ref, b0, b1, b2, b3, sems = scratch
+        along = lax.axis_index("along")
+        received = pltpu.make_async_copy(side_ref, out_ref.at[6:8], sems.at[1])
+        received.start()
+
+        @pl.when(along > 0)
         def _():
-            twice(reorder(back_ref[:height] - CENTRE, order_ref))
-            guide_stats(v2_ref.at[:, :height], (b0, b1, b2, b3), inv_ref, work_refs[0], work_refs[1])
-            for v in range(nv):
-                v2_ref[v, :height] = own_ref[v]
-                v2_ref[v, height:] = own_ref[v]
-            t = jnp.max(back_ref[height:, :LANES]).astype(i32)
-            side_partner(v2_ref, z_ref, t)
-            pair_maps(partner, (b0, b1, b2, b3), inv_ref, work_refs, maps_ref)
-            finish(1)
-
-        @pl.when(base_ref[2] == 0)
+            put(v_ref, reorder(back_ref[:height] - CENTRE, order_ref))
+            guide_stats(v_ref, (b0, b1, b2, b3), inv_ref, work_refs[0], work_refs[1])
+            forward_partner(own_ref, y_ref, jnp.max(back_ref[height:, :LANES]).astype(i32))
+            pair_maps(lambda j, k, d: y_ref[k + d, j], (b0, b1, b2, b3), inv_ref, work_refs, maps_ref)
+            finish(maps_ref, order_ref, res_ref, out_ref.at[2:4], sems.at[0]).wait()
+
+        @pl.when(along == 0)
         def _():
-            res_ref[1] = jnp.zeros(res_ref.shape[1:], f32)
-
-        send(1, 6)
-        for copy in copies:
+            res_ref[...] = jnp.zeros_like(res_ref)
+            copy = pltpu.make_async_copy(res_ref, out_ref.at[2:4], sems.at[0])
+            copy.start()
             copy.wait()
-
+        received.wait()
+
+    maps_shape = vmem(nv, 2 * height, LANES)
     fwd_image = shifted(images, "along", -1)
     side_image = shifted(images, "strip", -1)
-    scalars = jnp.concatenate([base, strip.astype(i32)[None]])
-    packed = call(
-        pack, (scalars, images), [IN_SMEM, IN_VMEM],
-        jax.ShapeDtypeStruct((height + SUBS, width), f32), IN_VMEM, [], 2**16, "pack",
-    )
-    back_image = shifted(packed, "strip", 1)
-    order, own, inv, *stats = call(
-        prepare, (images,), [IN_VMEM],
-        [jax.ShapeDtypeStruct((width, width), bf16), jax.ShapeDtypeStruct((nv, height, LANES), f32)] + [tile_field] * 5,
-        [IN_VMEM] * 7, [vmem(*field(kk))] * 2, 2**26, "prepare",
-    )
-    fwd_image, side_image, back_image = lax.optimization_barrier((fwd_image, side_image, back_image))
-    maps_shape = vmem(nv, 2 * height, LANES)
-    fwd_maps = call(
-        forward, (scalars, fwd_image, order, inv, *stats), [IN_SMEM] + [IN_VMEM] * 7,
+    order, own, packed, inv, *stats = call(
+        prepare, (offsets, images), [IN_SMEM, IN_VMEM],
+        [jax.ShapeDtypeStruct((width, width), bf16), jax.ShapeDtypeStruct((nv, height, LANES), f32),
+         jax.ShapeDtypeStruct((height + SUBS, width), f32)] + [tile_field] * 5,
+        [IN_VMEM] * 8, [vmem(*field(kk))] * 2, 2**26, "prepare",
+    )
+    back_image = shifted(packed, "along", 1)
+    fwd_image, side_image = lax.optimization_barrier((fwd_image, side_image))
+    side_maps = call(
+        side, (offsets, side_image, order, inv, *stats), [IN_SMEM] + [IN_VMEM] * 7,
         jax.ShapeDtypeStruct((2, height, width), f32), IN_VMEM,
-        work + [vmem(nv, height, LANES), vmem(kk + 3, 8, SUBS, LANES), maps_shape], 2**28, "forward",
-    )
-    fwd_back = shifted(fwd_maps, "along", 1)
+        work + [maps_shape, vmem(8 + 3, kk, SUBS, LANES), maps_shape], 2**28, "side",
+    )
+    side_back = shifted(side_maps, "strip", 1)
+    pair_scratch = work + [vmem(nv, height, LANES), vmem(kk + 3, 8, SUBS, LANES), maps_shape, vmem(2, height, width)]
+    whole = jax.ShapeDtypeStruct((8, height, width), f32)
     out = call(
-        side, (scalars, own, back_image, side_image, order, inv, *stats, fwd_maps), [IN_SMEM] + [IN_VMEM] * 10,
-        jax.ShapeDtypeStruct((8, height, width), f32), IN_ANY,
-        work + [maps_shape, vmem(8 + 3, kk, SUBS, LANES), maps_shape, vmem(2, 2, height, width)]
-        + [vmem(*field(kk))] * 4 + [pltpu.SemaphoreType.DMA((3,))], 2**29, "side",
-    )
-    return lax.dynamic_update_slice(out, fwd_back, (2, 0, 0))
+        forward, (offsets, fwd_image, order, inv, *stats, side_maps), [IN_SMEM] + [IN_VMEM] * 8,
+        whole, IN_ANY, pair_scratch + [pltpu.SemaphoreType.DMA((2,))], 2**28, "forward",
+    )
+    return call(
+        backward, (own, back_image, order, inv, side_back, out), [IN_VMEM] * 5 + [IN_ANY],
+        whole, IN_ANY, pair_scratch + [vmem(*field(kk))] * 4 + [pltpu.SemaphoreType.DMA((2,))], 2**28, "backward", {5: 0},
+    )
 
 
 def solution(mesh):

time: 41.9 us -> 38.2 us (0.912)
  the two profiles are of different devices: /device:TPU:19 before, /device:TPU:1 now
where the time goes in v1:
time: 38.2 us; the launch traced here: 38 us
  Pallas kernels  23.7 us (62%)
  starting transfers between devices  10.7 us (28%)
  waiting for transfers between devices  2 us (5%)
  local copies, waits for them, and re-layouts  1.55 us (4%)
    pallas_call x4, Pallas kernels, call(): pl.pallas_call(body, in_specs=in_specs, out_specs=out_specs, out_shape=ou...  23.7 us
    ppermute x4, starting transfers between devices, shifted(): lax.ppermute(value, axis, [(i, i + steps) for i in range(max(0, -steps),...  10.7 us
    ppermute x4, waiting for transfers between devices, shifted(): lax.ppermute(value, axis, [(i, i + steps) for i in range(max(0, -steps),...  2 us
    unnamed x4, local copies, waits for them, and re-layouts  1.55 us
  transfers between devices with their start and end apart: 4, of which 2 were waited for; matrix products, arithmetic and copies ran while one was open for 0% of the time, Pallas kernels for 25%

profile of v1, /device:TPU:1, one launch (start us, length us, event | category | flops | bytes accessed | tf_op | source)
XLA Modules:
  0.0 38.0 jit_solution(832578184548067368)
XLA Ops:
  0.0 1.3 %collective-permute-start.2 = (f32[64,512]{1,0:T(8,128)}, f32[64,512]{1,0:T(8,128)S(1)}, u32[]{:S(2)}, u32[]{:S(2)}) collective-permute-start(f32[64,512]{1,0:T(8,128)} %image_ref.1), channel_id=1, source_target_pairs={{8,0},{16,8},{24,16},{9,1},{17,9},{25,17},{10,2},{18,10},{26,18},{... | collective-permute-start | bytes 393224 | tf_op jit(solution)/shard_map/ppermute | solution.py:274
  1.3 2.0 %collective-permute-start.1 = (f32[64,512]{1,0:T(8,128)}, f32[64,512]{1,0:T(8,128)S(1)}, u32[]{:S(2)}, u32[]{:S(2)}) collective-permute-start(f32[64,512]{1,0:T(8,128)} %image_ref.1), channel_id=1, source_target_pairs={{1,0},{2,1},{3,2},{4,3},{5,4},{6,5},{7,6},{9,8},{10,9},{11,10},{12... | collective-permute-start | bytes 393224 | tf_op jit(solution)/shard_map/ppermute | solution.py:274
  3.3 0.0 copy-start
  3.3 0.6 %copy-done = s32[1,1,2]{2,1,0:T(1,128)S(1)} copy-done((s32[1,1,2]{2,1,0:T(1,128)S(1)}, s32[1,1,2]{2,1,0:T(1,128)}, u32[]{:S(2)}) %copy-start) | copy-done | bytes 32
  3.9 0.0 copy-start.1
  3.9 0.9 %copy-done.1 = f32[64,512]{1,0:T(8,128)S(1)} copy-done((f32[64,512]{1,0:T(8,128)S(1)}, f32[64,512]{1,0:T(8,128)}, u32[]{:S(2)}) %copy-start.1) | copy-done | bytes 131096
  4.8 1.9 %prepare.1 = (bf16[512,512]{1,0:T(8,128)(2,1)S(1)}, f32[4,64,128]{2,1,0:T(8,128)S(1)}, f32[72,512]{1,0:T(8,128)S(1)}, f32[8,16,8,128]{3,2,1,0:T(8,128)S(1)}, f32...) custom-call(s32[1,1,2]{2,1,0:T(1,128)S(1)} %copy-done, ...), custom_call_target="tpu_custom_call" | custom-call | flops 67108864 | bytes 1048576 | tf_op jit(solution)/shard_map/prepare/pallas_call | solution.py:255
  6.7 0.6 %collective-permute-done.2.other_ref = f32[64,512]{1,0:T(8,128)S(1)} collective-permute-done((f32[64,512]{1,0:T(8,128)}, f32[64,512]{1,0:T(8,128)S(1)}, u32[]{:S(2)}, u32[]{:S(2)}) %collective-permute-start.2) | collective-permute-done | bytes 131104 | tf_op jit(solution)/shard_map/ppermute | solution.py:274
  7.4 1.4 %collective-permute-done.1.other_ref = f32[64,512]{1,0:T(8,128)S(1)} collective-permute-done((f32[64,512]{1,0:T(8,128)}, f32[64,512]{1,0:T(8,128)S(1)}, u32[]{:S(2)}, u32[]{:S(2)}) %collective-permute-start.1) | collective-permute-done | bytes 131104 | tf_op jit(solution)/shard_map/ppermute | solution.py:274
  8.7 6.9 %side.1.side_ref = f32[2,64,512]{2,1,0:T(8,128)S(1)} custom-call(s32[1,1,2]{2,1,0:T(1,128)S(1)} %copy-done, f32[64,512]{1,0:T(8,128)S(1)} %collective-permute-done.2.other_ref, bf16[512,512]{1,0:T(8,128)(2,1)S(1)} %get-tuple-element.17.order_ref, f32[8,16,8,128]{3,2,1,0:T(8,128)S(1)} %get-tuple-element.18.inv_ref, ...), custom_call_target="tpu_custom_call" | custom-call | flops 268435456 | bytes 1048576 | tf_op jit(solution)/shard_map/side/pallas_call | solution.py:255
  15.6 4.3 %collective-permute-start.3 = (f32[2,64,512]{2,1,0:T(8,128)S(1)}, f32[2,64,512]{2,1,0:T(8,128)S(1)}, u32[]{:S(2)}, u32[]{:S(2)}) collective-permute-start(f32[2,64,512]{2,1,0:T(8,128)S(1)} %side.1.side_ref), channel_id=1, source_target_pairs={{0,8},{8,16},{16,24},{1,9},{9,17},{17,25},{2,10},{10,18},{18,26},{... | collective-permute-start | bytes 786440 | tf_op jit(solution)/shard_map/ppermute | solution.py:274
  19.9 3.2 %collective-permute-start = (f32[72,512]{1,0:T(8,128)S(1)}, f32[72,512]{1,0:T(8,128)S(1)}, u32[]{:S(2)}, u32[]{:S(2)}) collective-permute-start(f32[72,512]{1,0:T(8,128)S(1)} %get-tuple-element.16), channel_id=1, source_target_pairs={{0,1},{1,2},{2,3},{3,4},{4,5},{5,6},{6,7},{8,9},{9,10},{10,11},{11... | collective-permute-start | bytes 442376 | tf_op jit(solution)/shard_map/ppermute | solution.py:274
  23.2 7.4 %forward.1.old_ref = f32[8,64,512]{2,1,0:T(8,128)} custom-call(s32[1,1,2]{2,1,0:T(1,128)S(1)} %copy-done, f32[64,512]{1,0:T(8,128)S(1)} %collective-permute-done.1.other_ref, bf16[512,512]{1,0:T(8,128)(2,1)S(1)} %get-tuple-element.17.order_ref, f32[8,16,8,128]{3,2,1,0:T(8,128)S(1)} %get-tuple-element.18.inv_ref, ...), custom_call_target="tpu_custom_call" | custom-call | flops 268435456 | bytes 1048576 | tf_op jit(solution)/shard_map/forward/pallas_call | solution.py:255
  30.6 0.0 collective-permute-done.back_ref
  30.6 0.0 collective-permute-done.3.side_ref
  30.6 7.4 %backward.1 = f32[8,64,512]{2,1,0:T(8,128)} custom-call(f32[4,64,128]{2,1,0:T(8,128)S(1)} %get-tuple-element.15.own_ref, f32[72,512]{1,0:T(8,128)S(1)} %collective-permute-done.back_ref, bf16[512,512]{1,0:T(8,128)(2,1)S(1)} %get-tuple-element.17.order_ref, f32[8,16,8,128]{3,2,1,0:T(8,128)S(1)} %get-tuple-element.18.inv_ref, ...), custom_call_target="tpu_custom_call", output_to_operand_aliasing={{}: (5, {})} | custom-call | flops 268435456 | bytes 1048576 | tf_op jit(solution)/shard_map/backward/pallas_call | solution.py:255
Async XLA Ops:
  0.0 7.4 %collective-permute-start.2 = (f32[64,512]{1,0:T(8,128)}, f32[64,512]{1,0:T(8,128)S(1)}, u32[]{:S(2)}, u32[]{:S(2)}) collective-permute-start(f32[64,512]{1,0:T(8,128)} %image_ref.1), channel_id=1, source_target_pairs={{8,0},{16,8},{24,16},{9,1},{17,9},{25,17},{10,2},{18,10},{26,18},{... | collective-permute-start | bytes 393224 | tf_op jit(solution)/shard_map/ppermute | solution.py:274
  1.3 7.4 %collective-permute-start.1 = (f32[64,512]{1,0:T(8,128)}, f32[64,512]{1,0:T(8,128)S(1)}, u32[]{:S(2)}, u32[]{:S(2)}) collective-permute-start(f32[64,512]{1,0:T(8,128)} %image_ref.1), channel_id=1, source_target_pairs={{1,0},{2,1},{3,2},{4,3},{5,4},{6,5},{7,6},{9,8},{10,9},{11,10},{12... | collective-permute-start | bytes 393224 | tf_op jit(solution)/shard_map/ppermute | solution.py:274
  3.3 0.7 %copy-start = (s32[1,1,2]{2,1,0:T(1,128)S(1)}, s32[1,1,2]{2,1,0:T(1,128)}, u32[]{:S(2)}) copy-start(s32[1,1,2]{2,1,0:T(1,128)} %base_ref.5) | copy-start | bytes 28
  3.9 0.9 %copy-start.1 = (f32[64,512]{1,0:T(8,128)S(1)}, f32[64,512]{1,0:T(8,128)}, u32[]{:S(2)}) copy-start(f32[64,512]{1,0:T(8,128)} %image_ref.1) | copy-start | bytes 393220
  15.6 14.9 %collective-permute-start.3 = (f32[2,64,512]{2,1,0:T(8,128)S(1)}, f32[2,64,512]{2,1,0:T(8,128)S(1)}, u32[]{:S(2)}, u32[]{:S(2)}) collective-permute-start(f32[2,64,512]{2,1,0:T(8,128)S(1)} %side.1.side_ref), channel_id=1, source_target_pairs={{0,8},{8,16},{16,24},{1,9},{9,17},{17,25},{2,10},{10,18},{18,26},{... | collective-permute-start | bytes 786440 | tf_op jit(solution)/shard_map/ppermute | solution.py:274
  19.9 10.6 %collective-permute-start = (f32[72,512]{1,0:T(8,128)S(1)}, f32[72,512]{1,0:T(8,128)S(1)}, u32[]{:S(2)}, u32[]{:S(2)}) collective-permute-start(f32[72,512]{1,0:T(8,128)S(1)} %get-tuple-element.16), channel_id=1, source_target_pairs={{0,1},{1,2},{2,3},{3,4},{4,5},{5,6},{6,7},{8,9},{9,10},{10,11},{11... | collective-permute-start | bytes 442376 | tf_op jit(solution)/shard_map/ppermute | solution.py:274

commit v2 on v1

--- a/solution.py
+++ b/solution.py
@@ -273,13 +273,16 @@
         n = lax.axis_size(axis)
         return lax.ppermute(value, axis, [(i, i + steps) for i in range(max(0, -steps), min(n, n - steps))])
 
-    def prepare(base_ref, image_ref, order_ref, v_ref, packed_ref, inv_ref, g_ref, a1_ref, a2_ref, mean_ref, p_ref, q_ref):
-        packed_ref[:height] = image_ref[...]
-        packed_ref[height:] = jnp.full((SUBS, width), base_ref[0, 0, 0].astype(f32))
+    def prepare(base_ref, image_ref, order_ref, inv_ref, g_ref, a1_ref, a2_ref, mean_ref, v_ref, p_ref, q_ref):
         make_order(order_ref)
         inverse_counts(inv_ref, height, width)
         put(v_ref, reorder(image_ref[...] - CENTRE, order_ref))
         guide_stats(v_ref, (g_ref, a1_ref, a2_ref, mean_ref), inv_ref, p_ref, q_ref)
+
+    def finish(maps_ref, order_ref, out_ref):
+        maps = restore(maps_ref, order_ref)
+        out_ref[0] = maps[:height]
+        out_ref[1] = maps[height:]
 
     def side(base_ref, other_ref, order_ref, inv_ref, g_ref, a1_ref, a2_ref, mean_ref, out_ref, *scratch):
         *work_refs, v2_ref, z_ref, maps_ref = scratch
@@ -287,76 +290,50 @@
         put(v2_ref, jnp.concatenate([x, x]))
         side_partner(v2_ref, z_ref, base_ref[0, 0, 1])
         pair_maps(lambda j, k, d: z_ref[j + d, k], (g_ref, a1_ref, a2_ref, mean_ref), inv_ref, work_refs, maps_ref)
-        maps = restore(maps_ref, order_ref)
-        out_ref[0] = maps[:height]
-        out_ref[1] = maps[height:]
-
-    def finish(maps_ref, order_ref, res_ref, out_ref, sem):
-        maps = restore(maps_ref, order_ref)
-        res_ref[0] = maps[:height]
-        res_ref[1] = maps[height:]
-        copy = pltpu.make_async_copy(res_ref, out_ref, sem)
-        copy.start()
-        return copy
-
-    def forward(base_ref, other_ref, order_ref, inv_ref, g_ref, a1_ref, a2_ref, mean_ref, side_ref, out_ref, *scratch):
-        *work_refs, v_ref, y_ref, maps_ref, res_ref, sems = scratch
-        copy = pltpu.make_async_copy(side_ref, out_ref.at[4:6], sems.at[0])
-        copy.start()
+        finish(maps_ref, order_ref, out_ref)
+
+    def forward(base_ref, other_ref, order_ref, inv_ref, g_ref, a1_ref, a2_ref, mean_ref, out_ref, *scratch):
+        *work_refs, v_ref, y_ref, maps_ref = scratch
         put(v_ref, reorder(other_ref[...] - CENTRE, order_ref))
         forward_partner(v_ref, y_ref, base_ref[0, 0, 0])
         pair_maps(lambda j, k, d: y_ref[k + d, j], (g_ref, a1_ref, a2_ref, mean_ref), inv_ref, work_refs, maps_ref)
-        finish(maps_ref, order_ref, res_ref, out_ref.at[0:2], sems.at[1]).wait()
-        copy.wait()
-
-    def backward(own_ref, back_ref, order_ref, inv_ref, side_ref, old_ref, out_ref, *scratch):
-        *work_refs, v_ref, y_ref, maps_ref, res_ref, b0, b1, b2, b3, sems = scratch
-        along = lax.axis_index("along")
-        received = pltpu.make_async_copy(side_ref, out_ref.at[6:8], sems.at[1])
-        received.start()
-
-        @pl.when(along > 0)
-        def _():
-            put(v_ref, reorder(back_ref[:height] - CENTRE, order_ref))
-            guide_stats(v_ref, (b0, b1, b2, b3), inv_ref, work_refs[0], work_refs[1])
-            forward_partner(own_ref, y_ref, jnp.max(back_ref[height:, :LANES]).astype(i32))
-            pair_maps(lambda j, k, d: y_ref[k + d, j], (b0, b1, b2, b3), inv_ref, work_refs, maps_ref)
-            finish(maps_ref, order_ref, res_ref, out_ref.at[2:4], sems.at[0]).wait()
-
-        @pl.when(along == 0)
-        def _():
-            res_ref[...] = jnp.zeros_like(res_ref)
-            copy = pltpu.make_async_copy(res_ref, out_ref.at[2:4], sems.at[0])
+        finish(maps_ref, order_ref, out_ref)
+
+    def collect(rows, *refs):
+        out_ref, sems = refs[-2:]
+        copies = [pltpu.make_async_copy(refs[i], out_ref.at[row:row + 2], sems.at[i]) for i, row in enumerate(rows)]
+        for copy in copies:
             copy.start()
+        for copy in copies:
             copy.wait()
-        received.wait()
 
     maps_shape = vmem(nv, 2 * height, LANES)
+    two_maps = jax.ShapeDtypeStruct((2, height, width), f32)
+    whole = jax.ShapeDtypeStruct((8, height, width), f32)
     fwd_image = shifted(images, "along", -1)
     side_image = shifted(images, "strip", -1)
-    order, own, packed, inv, *stats = call(
-        prepare, (offsets, images), [IN_SMEM, IN_VMEM],
-        [jax.ShapeDtypeStruct((width, width), bf16), jax.ShapeDtypeStruct((nv, height, LANES), f32),
-         jax.ShapeDtypeStruct((height + SUBS, width), f32)] + [tile_field] * 5,
-        [IN_VMEM] * 8, [vmem(*field(kk))] * 2, 2**26, "prepare",
-    )
-    back_image = shifted(packed, "along", 1)
-    fwd_image, side_image = lax.optimization_barrier((fwd_image, side_image))
+    order, inv, *stats = call(
+        prepare, (offsets, images), [IN_SMEM, IN_VMEM], [jax.ShapeDtypeStruct((width, width), bf16)] + [tile_field] * 5,
+        [IN_VMEM] * 6, [vmem(nv, height, LANES)] + [vmem(*field(kk))] * 2, 2**26, "prepare",
+    )
+    side_image, fwd_image = lax.optimization_barrier((side_image, fwd_image))
     side_maps = call(
-        side, (offsets, side_image, order, inv, *stats), [IN_SMEM] + [IN_VMEM] * 7,
-        jax.ShapeDtypeStruct((2, height, width), f32), IN_VMEM,
+        side, (offsets, side_image, order, inv, *stats), [IN_SMEM] + [IN_VMEM] * 7, two_maps, IN_VMEM,
         work + [maps_shape, vmem(8 + 3, kk, SUBS, LANES), maps_shape], 2**28, "side",
     )
     side_back = shifted(side_maps, "strip", 1)
-    pair_scratch = work + [vmem(nv, height, LANES), vmem(kk + 3, 8, SUBS, LANES), maps_shape, vmem(2, height, width)]
-    whole = jax.ShapeDtypeStruct((8, height, width), f32)
+    fwd_maps = call(
+        forward, (offsets, fwd_image, order, inv, *stats), [IN_SMEM] + [IN_VMEM] * 7, two_maps, IN_VMEM,
+        work + [vmem(nv, height, LANES), vmem(kk + 3, 8, SUBS, LANES), maps_shape], 2**28, "forward",
+    )
+    fwd_back = shifted(fwd_maps, "along", 1)
     out = call(
-        forward, (offsets, fwd_image, order, inv, *stats, side_maps), [IN_SMEM] + [IN_VMEM] * 8,
-        whole, IN_ANY, pair_scratch + [pltpu.SemaphoreType.DMA((2,))], 2**28, "forward",
+        functools.partial(collect, (0, 4, 6)), (fwd_maps, side_maps, side_back), [IN_VMEM] * 3, whole, IN_ANY,
+        [pltpu.SemaphoreType.DMA((3,))], 2**20, "collect",
     )
     return call(
-        backward, (own, back_image, order, inv, side_back, out), [IN_VMEM] * 5 + [IN_ANY],
-        whole, IN_ANY, pair_scratch + [vmem(*field(kk))] * 4 + [pltpu.SemaphoreType.DMA((2,))], 2**28, "backward", {5: 0},
+        functools.partial(collect, (2,)), (fwd_back, out), [IN_VMEM, IN_ANY], whole, IN_ANY,
+        [pltpu.SemaphoreType.DMA((1,))], 2**20, "complete", {1: 0},
     )
 
 

time: 38.2 us -> 34.4 us (0.901); the launches traced: 38 us -> 33.8 us
  Pallas kernels: 23.7 us -> 17.1 us
  waiting for transfers between devices: 2 us -> 4.37 us
    pallas_call x4 -> x5, Pallas kernels: 23.7 us -> 17.1 us  [call(): pl.pallas_call(body, in_specs=in_specs, out_specs=out_specs, out_shape=ou...]
    ppermute x4, waiting for transfers between devices: 2 us -> 4.37 us  [shifted(): lax.ppermute(value, axis, [(i, i + steps) for i in range(max(0, -steps),...]
  transfers between devices with their start and end apart: 4 -> 4, of which waited for: 2 -> 3; matrix products, arithmetic and copies ran while one was open for 0% -> 0% of each run, Pallas kernels for 25% -> 28%
where the time goes in v2:
time: 34.4 us; the launch traced here: 33.8 us
  Pallas kernels  17.1 us (50%)
  starting transfers between devices  10.8 us (31%)
  waiting for transfers between devices  4.37 us (13%)
  local copies, waits for them, and re-layouts  1.55 us (5%)
    pallas_call x5, Pallas kernels, call(): pl.pallas_call(body, in_specs=in_specs, out_specs=out_specs, out_shape=ou...  17.1 us
    ppermute x4, starting transfers between devices, shifted(): lax.ppermute(value, axis, [(i, i + steps) for i in range(max(0, -steps),...  10.8 us
    ppermute x4, waiting for transfers between devices, shifted(): lax.ppermute(value, axis, [(i, i + steps) for i in range(max(0, -steps),...  4.37 us
    unnamed x4, local copies, waits for them, and re-layouts  1.55 us
  transfers between devices with their start and end apart: 4, of which 3 were waited for; matrix products, arithmetic and copies ran while one was open for 0% of the time, Pallas kernels for 28%

profile of v2, /device:TPU:1, one launch (start us, length us, event | category | flops | bytes accessed | tf_op | source)
XLA Modules:
  0.0 33.8 jit_solution(1463886643670208399)
XLA Ops:
  0.0 1.3 %collective-permute-start = (f32[64,512]{1,0:T(8,128)}, f32[64,512]{1,0:T(8,128)S(1)}, u32[]{:S(2)}, u32[]{:S(2)}) collective-permute-start(f32[64,512]{1,0:T(8,128)} %image_ref.1), channel_id=1, source_target_pairs={{8,0},{16,8},{24,16},{9,1},{17,9},{25,17},{10,2},{18,10},{26,18},{... | collective-permute-start | bytes 393224 | tf_op jit(solution)/shard_map/ppermute | solution.py:274
  1.3 2.0 %collective-permute-start.1 = (f32[64,512]{1,0:T(8,128)}, f32[64,512]{1,0:T(8,128)S(1)}, u32[]{:S(2)}, u32[]{:S(2)}) collective-permute-start(f32[64,512]{1,0:T(8,128)} %image_ref.1), channel_id=1, source_target_pairs={{1,0},{2,1},{3,2},{4,3},{5,4},{6,5},{7,6},{9,8},{10,9},{11,10},{12... | collective-permute-start | bytes 393224 | tf_op jit(solution)/shard_map/ppermute | solution.py:274
  3.3 0.0 copy-start
  3.3 0.6 %copy-done = s32[1,1,2]{2,1,0:T(1,128)S(1)} copy-done((s32[1,1,2]{2,1,0:T(1,128)S(1)}, s32[1,1,2]{2,1,0:T(1,128)}, u32[]{:S(2)}) %copy-start) | copy-done | bytes 32
  3.9 0.0 copy-start.1
  3.9 0.9 %copy-done.1 = f32[64,512]{1,0:T(8,128)S(1)} copy-done((f32[64,512]{1,0:T(8,128)S(1)}, f32[64,512]{1,0:T(8,128)}, u32[]{:S(2)}) %copy-start.1) | copy-done | bytes 131096
  4.8 1.9 %prepare.1 = (bf16[512,512]{1,0:T(8,128)(2,1)S(1)}, f32[8,16,8,128]{3,2,1,0:T(8,128)S(1)}, f32[8,16,8,128]{3,2,1,0:T(8,128)S(1)}, f32[8,16,8,128]{3,2,1,0:T(8,12...) custom-call(s32[1,1,2]{2,1,0:T(1,128)S(1)} %copy-done, f32[64,512]{1,0:T(8,128)S(1)} %copy-done.1), custom_call_target="tpu_custom_call" | custom-call | flops 67108864 | bytes 1048576 | tf_op jit(solution)/shard_map/prepare/pallas_call | solution.py:255
  6.7 0.6 %collective-permute-done.other_ref = f32[64,512]{1,0:T(8,128)S(1)} collective-permute-done((f32[64,512]{1,0:T(8,128)}, f32[64,512]{1,0:T(8,128)S(1)}, u32[]{:S(2)}, u32[]{:S(2)}) %collective-permute-start) | collective-permute-done | bytes 131104 | tf_op jit(solution)/shard_map/ppermute | solution.py:274
  7.4 1.4 %collective-permute-done.1.other_ref = f32[64,512]{1,0:T(8,128)S(1)} collective-permute-done((f32[64,512]{1,0:T(8,128)}, f32[64,512]{1,0:T(8,128)S(1)}, u32[]{:S(2)}, u32[]{:S(2)}) %collective-permute-start.1) | collective-permute-done | bytes 131104 | tf_op jit(solution)/shard_map/ppermute | solution.py:274
  8.7 6.9 %side.1.refs_1_ = f32[2,64,512]{2,1,0:T(8,128)S(1)} custom-call(s32[1,1,2]{2,1,0:T(1,128)S(1)} %copy-done, f32[64,512]{1,0:T(8,128)S(1)} %collective-permute-done.other_ref, bf16[512,512]{1,0:T(8,128)(2,1)S(1)} %get-tuple-element.14.order_ref, f32[8,16,8,128]{3,2,1,0:T(8,128)S(1)} %get-tuple-element.15.inv_ref, ...), custom_call_target="tpu_custom_call" | custom-call | flops 268435456 | bytes 1048576 | tf_op jit(solution)/shard_map/side/pallas_call | solution.py:255
  15.6 4.3 %collective-permute-start.3 = (f32[2,64,512]{2,1,0:T(8,128)S(1)}, f32[2,64,512]{2,1,0:T(8,128)S(1)}, u32[]{:S(2)}, u32[]{:S(2)}) collective-permute-start(f32[2,64,512]{2,1,0:T(8,128)S(1)} %side.1.refs_1_), channel_id=1, source_target_pairs={{0,8},{8,16},{16,24},{1,9},{9,17},{17,25},{2,10},{10,18},{18,26},{... | collective-permute-start | bytes 786440 | tf_op jit(solution)/shard_map/ppermute | solution.py:274
  19.9 6.7 %forward.1.refs_0_ = f32[2,64,512]{2,1,0:T(8,128)S(1)} custom-call(s32[1,1,2]{2,1,0:T(1,128)S(1)} %copy-done, f32[64,512]{1,0:T(8,128)S(1)} %collective-permute-done.1.other_ref, bf16[512,512]{1,0:T(8,128)(2,1)S(1)} %get-tuple-element.14.order_ref, f32[8,16,8,128]{3,2,1,0:T(8,128)S(1)} %get-tuple-element.15.inv_ref, ...), custom_call_target="tpu_custom_call" | custom-call | flops 268435456 | bytes 1048576 | tf_op jit(solution)/shard_map/forward/pallas_call | solution.py:255
  26.6 3.2 %collective-permute-start.2 = (f32[2,64,512]{2,1,0:T(8,128)S(1)}, f32[2,64,512]{2,1,0:T(8,128)S(1)}, u32[]{:S(2)}, u32[]{:S(2)}) collective-permute-start(f32[2,64,512]{2,1,0:T(8,128)S(1)} %forward.1.refs_0_), channel_id=1, source_target_pairs={{0,1},{1,2},{2,3},{3,4},{4,5},{5,6},{6,7},{8,9},{9,10},{10,11},{11... | collective-permute-start | bytes 786440 | tf_op jit(solution)/shard_map/ppermute | solution.py:274
  29.8 0.0 collective-permute-done.3.refs_2_
  29.9 0.9 %collect.1.refs_1_ = f32[8,64,512]{2,1,0:T(8,128)} custom-call(f32[2,64,512]{2,1,0:T(8,128)S(1)} %forward.1.refs_0_, f32[2,64,512]{2,1,0:T(8,128)S(1)} %side.1.refs_1_, f32[2,64,512]{2,1,0:T(8,128)S(1)} %collective-permute-done.3.refs_2_), custom_call_target="tpu_custom_call" | custom-call | flops 1048576 | bytes 1048576 | tf_op jit(solution)/shard_map/collect/pallas_call | solution.py:255
  30.8 2.4 %collective-permute-done.2.refs_0_ = f32[2,64,512]{2,1,0:T(8,128)S(1)} collective-permute-done((f32[2,64,512]{2,1,0:T(8,128)S(1)}, f32[2,64,512]{2,1,0:T(8,128)S(1)}, u32[]{:S(2)}, u32[]{:S(2)}) %collective-permute-start.2) | collective-permute-done | bytes 262176 | tf_op jit(solution)/shard_map/ppermute | solution.py:274
  33.1 0.7 %complete.1 = f32[8,64,512]{2,1,0:T(8,128)} custom-call(f32[2,64,512]{2,1,0:T(8,128)S(1)} %collective-permute-done.2.refs_0_, f32[8,64,512]{2,1,0:T(8,128)} %collect.1.refs_1_), custom_call_target="tpu_custom_call", output_to_operand_aliasing={{}: (1, {})} | custom-call | flops 1048576 | bytes 1048576 | tf_op jit(solution)/shard_map/complete/pallas_call | solution.py:255
Async XLA Ops:
  0.0 7.4 %collective-permute-start = (f32[64,512]{1,0:T(8,128)}, f32[64,512]{1,0:T(8,128)S(1)}, u32[]{:S(2)}, u32[]{:S(2)}) collective-permute-start(f32[64,512]{1,0:T(8,128)} %image_ref.1), channel_id=1, source_target_pairs={{8,0},{16,8},{24,16},{9,1},{17,9},{25,17},{10,2},{18,10},{26,18},{... | collective-permute-start | bytes 393224 | tf_op jit(solution)/shard_map/ppermute | solution.py:274
  1.3 7.4 %collective-permute-start.1 = (f32[64,512]{1,0:T(8,128)}, f32[64,512]{1,0:T(8,128)S(1)}, u32[]{:S(2)}, u32[]{:S(2)}) collective-permute-start(f32[64,512]{1,0:T(8,128)} %image_ref.1), channel_id=1, source_target_pairs={{1,0},{2,1},{3,2},{4,3},{5,4},{6,5},{7,6},{9,8},{10,9},{11,10},{12... | collective-permute-start | bytes 393224 | tf_op jit(solution)/shard_map/ppermute | solution.py:274
  3.3 0.7 %copy-start = (s32[1,1,2]{2,1,0:T(1,128)S(1)}, s32[1,1,2]{2,1,0:T(1,128)}, u32[]{:S(2)}) copy-start(s32[1,1,2]{2,1,0:T(1,128)} %base_ref.5) | copy-start | bytes 28
  3.9 0.9 %copy-start.1 = (f32[64,512]{1,0:T(8,128)S(1)}, f32[64,512]{1,0:T(8,128)}, u32[]{:S(2)}) copy-start(f32[64,512]{1,0:T(8,128)} %image_ref.1) | copy-start | bytes 393220
  15.6 14.2 %collective-permute-start.3 = (f32[2,64,512]{2,1,0:T(8,128)S(1)}, f32[2,64,512]{2,1,0:T(8,128)S(1)}, u32[]{:S(2)}, u32[]{:S(2)}) collective-permute-start(f32[2,64,512]{2,1,0:T(8,128)S(1)} %side.1.refs_1_), channel_id=1, source_target_pairs={{0,8},{8,16},{16,24},{1,9},{9,17},{17,25},{2,10},{10,18},{18,26},{... | collective-permute-start | bytes 786440 | tf_op jit(solution)/shard_map/ppermute | solution.py:274
  26.6 6.5 %collective-permute-start.2 = (f32[2,64,512]{2,1,0:T(8,128)S(1)}, f32[2,64,512]{2,1,0:T(8,128)S(1)}, u32[]{:S(2)}, u32[]{:S(2)}) collective-permute-start(f32[2,64,512]{2,1,0:T(8,128)S(1)} %forward.1.refs_0_), channel_id=1, source_target_pairs={{0,1},{1,2},{2,3},{3,4},{4,5},{5,6},{6,7},{8,9},{9,10},{10,11},{11... | collective-permute-start | bytes 786440 | tf_op jit(solution)/shard_map/ppermute | solution.py:274

commit v3 on v2

--- a/solution.py
+++ b/solution.py
@@ -83,10 +83,10 @@
 
 def put(ref, x):
     for v in range(ref.shape[0]):
-        ref[v] = x[:, v * LANES:(v + 1) * LANES]
-
-
-def inverse_counts(inv_ref, height, width):
+        ref[v, :x.shape[0]] = x[:, v * LANES:(v + 1) * LANES]
+
+
+def inverse_counts(inv_ref, scale_ref, height, width):
     lane, sub = iota(1), iota(0)
     kk = inv_ref.shape[1]
     count = lambda i, n: 1.0 / (jnp.minimum(i + RADIUS, n - 1) - jnp.maximum(i - RADIUS, 0) + 1).astype(f32)
@@ -94,7 +94,9 @@
     for j in range(8):
         row = count(sub * 8 + j, height)
         for k in range(kk):
-            inv_ref[j, k] = row * cols[k]
+            inv = row * cols[k]
+            inv_ref[j, k] = inv
+            scale_ref[j, k] = inv * (-4.0 * math.log2(math.e))
 
 
 def guide_stats(v_ref, stats, inv_ref, p_ref, q_ref):
@@ -142,7 +144,7 @@
 
 
 def side_partner(v2_ref, z_ref, t):
-    nv, height = v2_ref.shape[0], v2_ref.shape[1] // 2
+    nv, height = v2_ref.shape[0], (v2_ref.shape[1] - SUBS) // 2
     odd, upper = iota(1) % 2 == 1, iota(1) % GROUP >= 2
 
     def one(m):
@@ -164,39 +166,50 @@
 
 
 def pair_maps(partner, stats, inv_ref, work, out_ref):
-    g_ref, a1_ref, a2_ref, mean_ref = stats
-    p_ref, q_ref, a_ref, b_ref, score_ref = work
+    g_ref, a1_ref, a2_ref, mean_ref, scale_ref = stats
+    p2_ref, q2_ref, a2w_ref, b2_ref, score_ref = work
     kk = g_ref.shape[1]
     levels = DISP // GROUP
 
-    def level(d):
-        def first(j):
-            g = [g_ref[j, k] for k in range(kk)]
-            cost = [jnp.abs(g[k] - partner(j, k, d)) for k in range(kk)]
-            for k, y in enumerate(box_cols(cost)):
-                p_ref[j, k] = y
-            for k, y in enumerate(box_cols([x * y for x, y in zip(g, cost)])):
-                q_ref[j, k] = y
-        loop(8, first)
-
-        def second(k):
-            p = box_rows([p_ref[j, k] for j in range(8)])
-            q = box_rows([q_ref[j, k] for j in range(8)])
-            ca = [q[j] * a1_ref[j, k] - p[j] * a2_ref[j, k] for j in range(8)]
-            cb = [p[j] * inv_ref[j, k] - ca[j] * mean_ref[j, k] for j in range(8)]
-            for j, y in enumerate(box_rows(ca)):
-                a_ref[j, k] = y
-            for j, y in enumerate(box_rows(cb)):
-                b_ref[j, k] = y
-        loop(kk, second)
-
-        def third(j):
-            a = box_cols([a_ref[j, k] for k in range(kk)])
-            b = box_cols([b_ref[j, k] for k in range(kk)])
-            for k in range(kk):
-                score_ref[d, j, k] = (a[k] * g_ref[j, k] + b[k]) * (inv_ref[j, k] * (-4.0 * math.log2(math.e)))
-        loop(8, third)
-    loop(levels, level, 1)
+    def first(d, e, j):
+        g = [g_ref[j, k] for k in range(kk)]
+        cost = [jnp.abs(g[k] - partner(j, k, d)) for k in range(kk)]
+        for k, y in enumerate(box_cols(cost)):
+            p2_ref[e, j, k] = y
+        for k, y in enumerate(box_cols([x * y for x, y in zip(g, cost)])):
+            q2_ref[e, j, k] = y
+
+    def second(e, k):
+        p = box_rows([p2_ref[e, j, k] for j in range(8)])
+        q = box_rows([q2_ref[e, j, k] for j in range(8)])
+        ca = [q[j] * a1_ref[j, k] - p[j] * a2_ref[j, k] for j in range(8)]
+        cb = [p[j] * inv_ref[j, k] - ca[j] * mean_ref[j, k] for j in range(8)]
+        for j, y in enumerate(box_rows(ca)):
+            a2w_ref[e, j, k] = y
+        for j, y in enumerate(box_rows(cb)):
+            b2_ref[e, j, k] = y
+
+    def third(d, e, j):
+        a = box_cols([a2w_ref[e, j, k] for k in range(kk)])
+        b = box_cols([b2_ref[e, j, k] for k in range(kk)])
+        for k in range(kk):
+            score_ref[d, j, k] = (a[k] * g_ref[j, k] + b[k]) * scale_ref[j, k]
+
+    def levels2(n):
+        d = 2 * n
+        loop(8, lambda j: first(d, 0, j))
+        for i in range(8):
+            first(d + 1, 1, i)
+            second(0, 2 * i)
+            second(0, 2 * i + 1)
+        for i in range(8):
+            third(d, 0, i)
+            second(1, 2 * i)
+            second(1, 2 * i + 1)
+        loop(8, lambda j: third(d + 1, 1, j))
+    loop(levels // 2, levels2, 1)
+
+    p_ref, q_ref, a_ref, b_ref = p2_ref.at[0], q2_ref.at[0], a2w_ref.at[0], b2_ref.at[0]
 
     nv = kk // GROUP
     odd, upper = iota(1) % 2 == 1, iota(1) % GROUP >= 2
@@ -221,7 +234,7 @@
             p_ref[j, k] = s
             q_ref[j, k] = t + lane_level * s
             a_ref[j, k] = functools.reduce(jnp.add, [x * x for x in w])
-    loop(8, weights, 1)
+    loop(8, weights, 2)
 
     def halves(j):
         for v in range(nv):
@@ -231,7 +244,7 @@
                     ref[j, n // 2 * nv + v] = jnp.where(odd, x[n + 1], x[n]) + swap(jnp.where(odd, x[n], x[n + 1]), 1)
     loop(8, halves)
 
-    height = out_ref.shape[1] // 2
+    height = (out_ref.shape[1] - SUBS) // 2
 
     def last(j):
         for v in range(nv):
@@ -244,7 +257,8 @@
 
 
 def restore(out_ref, order_ref):
-    return reorder(jnp.concatenate([out_ref[v] for v in range(out_ref.shape[0])], axis=1), order_ref, back=True)
+    rows = out_ref.shape[1] - SUBS
+    return reorder(jnp.concatenate([out_ref[v, :rows] for v in range(out_ref.shape[0])], axis=1), order_ref, back=True)
 
 
 def field(kk, *lead):
@@ -267,15 +281,15 @@
     assert height == 8 * SUBS and kk == DISP
     tile_field = jax.ShapeDtypeStruct(field(kk), f32)
     vmem = lambda *shape: pltpu.VMEM(shape, f32)
-    work = [vmem(*field(kk))] * 4 + [vmem(*field(kk, DISP // GROUP))]
+    work = [vmem(*field(kk, 2))] * 4 + [vmem(*field(kk, DISP // GROUP))]
 
     def shifted(value, axis, steps):
         n = lax.axis_size(axis)
         return lax.ppermute(value, axis, [(i, i + steps) for i in range(max(0, -steps), min(n, n - steps))])
 
-    def prepare(base_ref, image_ref, order_ref, inv_ref, g_ref, a1_ref, a2_ref, mean_ref, v_ref, p_ref, q_ref):
+    def prepare(base_ref, image_ref, order_ref, inv_ref, g_ref, a1_ref, a2_ref, mean_ref, scale_ref, v_ref, p_ref, q_ref):
         make_order(order_ref)
-        inverse_counts(inv_ref, height, width)
+        inverse_counts(inv_ref, scale_ref, height, width)
         put(v_ref, reorder(image_ref[...] - CENTRE, order_ref))
         guide_stats(v_ref, (g_ref, a1_ref, a2_ref, mean_ref), inv_ref, p_ref, q_ref)
 
@@ -284,19 +298,19 @@
         out_ref[0] = maps[:height]
         out_ref[1] = maps[height:]
 
-    def side(base_ref, other_ref, order_ref, inv_ref, g_ref, a1_ref, a2_ref, mean_ref, out_ref, *scratch):
+    def side(base_ref, other_ref, order_ref, inv_ref, g_ref, a1_ref, a2_ref, mean_ref, scale_ref, out_ref, *scratch):
         *work_refs, v2_ref, z_ref, maps_ref = scratch
         x = reorder(other_ref[...] - CENTRE, order_ref)
         put(v2_ref, jnp.concatenate([x, x]))
         side_partner(v2_ref, z_ref, base_ref[0, 0, 1])
-        pair_maps(lambda j, k, d: z_ref[j + d, k], (g_ref, a1_ref, a2_ref, mean_ref), inv_ref, work_refs, maps_ref)
+        pair_maps(lambda j, k, d: z_ref[j + d, k], (g_ref, a1_ref, a2_ref, mean_ref, scale_ref), inv_ref, work_refs, maps_ref)
         finish(maps_ref, order_ref, out_ref)
 
-    def forward(base_ref, other_ref, order_ref, inv_ref, g_ref, a1_ref, a2_ref, mean_ref, out_ref, *scratch):
+    def forward(base_ref, other_ref, order_ref, inv_ref, g_ref, a1_ref, a2_ref, mean_ref, scale_ref, out_ref, *scratch):
         *work_refs, v_ref, y_ref, maps_ref = scratch
         put(v_ref, reorder(other_ref[...] - CENTRE, order_ref))
         forward_partner(v_ref, y_ref, base_ref[0, 0, 0])
-        pair_maps(lambda j, k, d: y_ref[k + d, j], (g_ref, a1_ref, a2_ref, mean_ref), inv_ref, work_refs, maps_ref)
+        pair_maps(lambda j, k, d: y_ref[k + d, j], (g_ref, a1_ref, a2_ref, mean_ref, scale_ref), inv_ref, work_refs, maps_ref)
         finish(maps_ref, order_ref, out_ref)
 
     def collect(rows, *refs):
@@ -307,24 +321,25 @@
         for copy in copies:
             copy.wait()
 
-    maps_shape = vmem(nv, 2 * height, LANES)
+    maps_shape = vmem(nv, 2 * height + SUBS, LANES)
+    image_shape = vmem(nv, height + SUBS, LANES)
     two_maps = jax.ShapeDtypeStruct((2, height, width), f32)
     whole = jax.ShapeDtypeStruct((8, height, width), f32)
     fwd_image = shifted(images, "along", -1)
     side_image = shifted(images, "strip", -1)
     order, inv, *stats = call(
-        prepare, (offsets, images), [IN_SMEM, IN_VMEM], [jax.ShapeDtypeStruct((width, width), bf16)] + [tile_field] * 5,
-        [IN_VMEM] * 6, [vmem(nv, height, LANES)] + [vmem(*field(kk))] * 2, 2**26, "prepare",
+        prepare, (offsets, images), [IN_SMEM, IN_VMEM], [jax.ShapeDtypeStruct((width, width), bf16)] + [tile_field] * 6,
+        [IN_VMEM] * 7, [image_shape] + [vmem(*field(kk))] * 2, 2**26, "prepare",
     )
     side_image, fwd_image = lax.optimization_barrier((side_image, fwd_image))
     side_maps = call(
-        side, (offsets, side_image, order, inv, *stats), [IN_SMEM] + [IN_VMEM] * 7, two_maps, IN_VMEM,
+        side, (offsets, side_image, order, inv, *stats), [IN_SMEM] + [IN_VMEM] * 8, two_maps, IN_VMEM,
         work + [maps_shape, vmem(8 + 3, kk, SUBS, LANES), maps_shape], 2**28, "side",
     )
     side_back = shifted(side_maps, "strip", 1)
     fwd_maps = call(
-        forward, (offsets, fwd_image, order, inv, *stats), [IN_SMEM] + [IN_VMEM] * 7, two_maps, IN_VMEM,
-        work + [vmem(nv, height, LANES), vmem(kk + 3, 8, SUBS, LANES), maps_shape], 2**28, "forward",
+        forward, (offsets, fwd_image, order, inv, *stats), [IN_SMEM] + [IN_VMEM] * 8, two_maps, IN_VMEM,
+        work + [image_shape, vmem(kk + 3, 8, SUBS, LANES), maps_shape], 2**28, "forward",
     )
     fwd_back = shifted(fwd_maps, "along", 1)
     out = call(

time: 34.4 us -> 34 us (0.988)
  Pallas kernels: 17.1 us -> 16.7 us
    pallas_call x5, Pallas kernels: 17.1 us -> 16.7 us  [call(): pl.pallas_call(body, in_specs=in_specs, out_specs=out_specs, out_shape=ou...]
where the time goes in v3:
time: 34 us; the launch traced here: 33.4 us
  Pallas kernels  16.7 us (49%)
  starting transfers between devices  10.7 us (31%)
  waiting for transfers between devices  4.34 us (13%)
  local copies, waits for them, and re-layouts  1.55 us (5%)
    pallas_call x5, Pallas kernels, call(): pl.pallas_call(body, in_specs=in_specs, out_specs=out_specs, out_shape=ou...  16.7 us
    ppermute x4, starting transfers between devices, shifted(): lax.ppermute(value, axis, [(i, i + steps) for i in range(max(0, -steps),...  10.7 us
    ppermute x4, waiting for transfers between devices, shifted(): lax.ppermute(value, axis, [(i, i + steps) for i in range(max(0, -steps),...  4.34 us
    unnamed x4, local copies, waits for them, and re-layouts  1.55 us
  transfers between devices with their start and end apart: 4, of which 3 were waited for; matrix products, arithmetic and copies ran while one was open for 0% of the time, Pallas kernels for 28%

profile of v3, /device:TPU:1, one launch (start us, length us, event | category | flops | bytes accessed | tf_op | source)
XLA Modules:
  0.0 33.4 jit_solution(8943776306473905503)
XLA Ops:
  0.0 1.3 %collective-permute-start = (f32[64,512]{1,0:T(8,128)}, f32[64,512]{1,0:T(8,128)S(1)}, u32[]{:S(2)}, u32[]{:S(2)}) collective-permute-start(f32[64,512]{1,0:T(8,128)} %image_ref.1), channel_id=1, source_target_pairs={{8,0},{16,8},{24,16},{9,1},{17,9},{25,17},{10,2},{18,10},{26,18},{... | collective-permute-start | bytes 393224 | tf_op jit(solution)/shard_map/ppermute | solution.py:288
  1.3 2.0 %collective-permute-start.1 = (f32[64,512]{1,0:T(8,128)}, f32[64,512]{1,0:T(8,128)S(1)}, u32[]{:S(2)}, u32[]{:S(2)}) collective-permute-start(f32[64,512]{1,0:T(8,128)} %image_ref.1), channel_id=1, source_target_pairs={{1,0},{2,1},{3,2},{4,3},{5,4},{6,5},{7,6},{9,8},{10,9},{11,10},{12... | collective-permute-start | bytes 393224 | tf_op jit(solution)/shard_map/ppermute | solution.py:288
  3.3 0.0 copy-start
  3.3 0.6 %copy-done = s32[1,1,2]{2,1,0:T(1,128)S(1)} copy-done((s32[1,1,2]{2,1,0:T(1,128)S(1)}, s32[1,1,2]{2,1,0:T(1,128)}, u32[]{:S(2)}) %copy-start) | copy-done | bytes 32
  3.9 0.0 copy-start.1
  3.9 0.9 %copy-done.1 = f32[64,512]{1,0:T(8,128)S(1)} copy-done((f32[64,512]{1,0:T(8,128)S(1)}, f32[64,512]{1,0:T(8,128)}, u32[]{:S(2)}) %copy-start.1) | copy-done | bytes 131096
  4.8 1.9 %prepare.1 = (bf16[512,512]{1,0:T(8,128)(2,1)S(1)}, f32[8,16,8,128]{3,2,1,0:T(8,128)S(1)}, f32[8,16,8,128]{3,2,1,0:T(8,128)S(1)}, f32[8,16,8,128]{3,2,1,0:T(8,12...) custom-call(s32[1,1,2]{2,1,0:T(1,128)S(1)} %copy-done, ...), custom_call_target="tpu_custom_call" | custom-call | flops 67108864 | bytes 1048576 | tf_op jit(solution)/shard_map/prepare/pallas_call | solution.py:269
  6.8 0.6 %collective-permute-done.other_ref = f32[64,512]{1,0:T(8,128)S(1)} collective-permute-done((f32[64,512]{1,0:T(8,128)}, f32[64,512]{1,0:T(8,128)S(1)}, u32[]{:S(2)}, u32[]{:S(2)}) %collective-permute-start) | collective-permute-done | bytes 131104 | tf_op jit(solution)/shard_map/ppermute | solution.py:288
  7.4 1.4 %collective-permute-done.1.other_ref = f32[64,512]{1,0:T(8,128)S(1)} collective-permute-done((f32[64,512]{1,0:T(8,128)}, f32[64,512]{1,0:T(8,128)S(1)}, u32[]{:S(2)}, u32[]{:S(2)}) %collective-permute-start.1) | collective-permute-done | bytes 131104 | tf_op jit(solution)/shard_map/ppermute | solution.py:288
  8.7 6.7 %side.1.refs_1_ = f32[2,64,512]{2,1,0:T(8,128)S(1)} custom-call(s32[1,1,2]{2,1,0:T(1,128)S(1)} %copy-done, f32[64,512]{1,0:T(8,128)S(1)} %collective-permute-done.other_ref, bf16[512,512]{1,0:T(8,128)(2,1)S(1)} %get-tuple-element.15.order_ref, f32[8,16,8,128]{3,2,1,0:T(8,128)S(1)} %get-tuple-element.16.inv_ref, ...), custom_call_target="tpu_custom_call" | custom-call | flops 268435456 | bytes 1048576 | tf_op jit(solution)/shard_map/side/pallas_call | solution.py:269
  15.4 4.3 %collective-permute-start.3 = (f32[2,64,512]{2,1,0:T(8,128)S(1)}, f32[2,64,512]{2,1,0:T(8,128)S(1)}, u32[]{:S(2)}, u32[]{:S(2)}) collective-permute-start(f32[2,64,512]{2,1,0:T(8,128)S(1)} %side.1.refs_1_), channel_id=1, source_target_pairs={{0,8},{8,16},{16,24},{1,9},{9,17},{17,25},{2,10},{10,18},{18,26},{... | collective-permute-start | bytes 786440 | tf_op jit(solution)/shard_map/ppermute | solution.py:288
  19.7 6.5 %forward.1.refs_0_ = f32[2,64,512]{2,1,0:T(8,128)S(1)} custom-call(s32[1,1,2]{2,1,0:T(1,128)S(1)} %copy-done, f32[64,512]{1,0:T(8,128)S(1)} %collective-permute-done.1.other_ref, bf16[512,512]{1,0:T(8,128)(2,1)S(1)} %get-tuple-element.15.order_ref, f32[8,16,8,128]{3,2,1,0:T(8,128)S(1)} %get-tuple-element.16.inv_ref, ...), custom_call_target="tpu_custom_call" | custom-call | flops 268435456 | bytes 1048576 | tf_op jit(solution)/shard_map/forward/pallas_call | solution.py:269
  26.2 3.2 %collective-permute-start.2 = (f32[2,64,512]{2,1,0:T(8,128)S(1)}, f32[2,64,512]{2,1,0:T(8,128)S(1)}, u32[]{:S(2)}, u32[]{:S(2)}) collective-permute-start(f32[2,64,512]{2,1,0:T(8,128)S(1)} %forward.1.refs_0_), channel_id=1, source_target_pairs={{0,1},{1,2},{2,3},{3,4},{4,5},{5,6},{6,7},{8,9},{9,10},{10,11},{11... | collective-permute-start | bytes 786440 | tf_op jit(solution)/shard_map/ppermute | solution.py:288
  29.4 0.0 collective-permute-done.3.refs_2_
  29.4 0.9 %collect.1.refs_1_ = f32[8,64,512]{2,1,0:T(8,128)} custom-call(f32[2,64,512]{2,1,0:T(8,128)S(1)} %forward.1.refs_0_, f32[2,64,512]{2,1,0:T(8,128)S(1)} %side.1.refs_1_, f32[2,64,512]{2,1,0:T(8,128)S(1)} %collective-permute-done.3.refs_2_), custom_call_target="tpu_custom_call" | custom-call | flops 1048576 | bytes 1048576 | tf_op jit(solution)/shard_map/collect/pallas_call | solution.py:269
  30.3 2.4 %collective-permute-done.2.refs_0_ = f32[2,64,512]{2,1,0:T(8,128)S(1)} collective-permute-done((f32[2,64,512]{2,1,0:T(8,128)S(1)}, f32[2,64,512]{2,1,0:T(8,128)S(1)}, u32[]{:S(2)}, u32[]{:S(2)}) %collective-permute-start.2) | collective-permute-done | bytes 262176 | tf_op jit(solution)/shard_map/ppermute | solution.py:288
  32.7 0.7 %complete.1 = f32[8,64,512]{2,1,0:T(8,128)} custom-call(f32[2,64,512]{2,1,0:T(8,128)S(1)} %collective-permute-done.2.refs_0_, f32[8,64,512]{2,1,0:T(8,128)} %collect.1.refs_1_), custom_call_target="tpu_custom_call", output_to_operand_aliasing={{}: (1, {})} | custom-call | flops 1048576 | bytes 1048576 | tf_op jit(solution)/shard_map/complete/pallas_call | solution.py:269
Async XLA Ops:
  0.0 7.4 %collective-permute-start = (f32[64,512]{1,0:T(8,128)}, f32[64,512]{1,0:T(8,128)S(1)}, u32[]{:S(2)}, u32[]{:S(2)}) collective-permute-start(f32[64,512]{1,0:T(8,128)} %image_ref.1), channel_id=1, source_target_pairs={{8,0},{16,8},{24,16},{9,1},{17,9},{25,17},{10,2},{18,10},{26,18},{... | collective-permute-start | bytes 393224 | tf_op jit(solution)/shard_map/ppermute | solution.py:288
  1.3 7.4 %collective-permute-start.1 = (f32[64,512]{1,0:T(8,128)}, f32[64,512]{1,0:T(8,128)S(1)}, u32[]{:S(2)}, u32[]{:S(2)}) collective-permute-start(f32[64,512]{1,0:T(8,128)} %image_ref.1), channel_id=1, source_target_pairs={{1,0},{2,1},{3,2},{4,3},{5,4},{6,5},{7,6},{9,8},{10,9},{11,10},{12... | collective-permute-start | bytes 393224 | tf_op jit(solution)/shard_map/ppermute | solution.py:288
  3.3 0.7 %copy-start = (s32[1,1,2]{2,1,0:T(1,128)S(1)}, s32[1,1,2]{2,1,0:T(1,128)}, u32[]{:S(2)}) copy-start(s32[1,1,2]{2,1,0:T(1,128)} %base_ref.5) | copy-start | bytes 28
  3.9 0.9 %copy-start.1 = (f32[64,512]{1,0:T(8,128)S(1)}, f32[64,512]{1,0:T(8,128)}, u32[]{:S(2)}) copy-start(f32[64,512]{1,0:T(8,128)} %image_ref.1) | copy-start | bytes 393220
  15.4 14.0 %collective-permute-start.3 = (f32[2,64,512]{2,1,0:T(8,128)S(1)}, f32[2,64,512]{2,1,0:T(8,128)S(1)}, u32[]{:S(2)}, u32[]{:S(2)}) collective-permute-start(f32[2,64,512]{2,1,0:T(8,128)S(1)} %side.1.refs_1_), channel_id=1, source_target_pairs={{0,8},{8,16},{16,24},{1,9},{9,17},{17,25},{2,10},{10,18},{18,26},{... | collective-permute-start | bytes 786440 | tf_op jit(solution)/shard_map/ppermute | solution.py:288
  26.2 6.5 %collective-permute-start.2 = (f32[2,64,512]{2,1,0:T(8,128)S(1)}, f32[2,64,512]{2,1,0:T(8,128)S(1)}, u32[]{:S(2)}, u32[]{:S(2)}) collective-permute-start(f32[2,64,512]{2,1,0:T(8,128)S(1)} %forward.1.refs_0_), channel_id=1, source_target_pairs={{0,1},{1,2},{2,3},{3,4},{4,5},{5,6},{6,7},{8,9},{9,10},{10,11},{11... | collective-permute-start | bytes 786440 | tf_op jit(solution)/shard_map/ppermute | solution.py:288

commit v4 on v3

--- a/solution.py
+++ b/solution.py
@@ -298,17 +298,23 @@
         out_ref[0] = maps[:height]
         out_ref[1] = maps[height:]
 
-    def side(base_ref, other_ref, order_ref, inv_ref, g_ref, a1_ref, a2_ref, mean_ref, scale_ref, out_ref, *scratch):
-        *work_refs, v2_ref, z_ref, maps_ref = scratch
+    def side(base_in, other_ref, order_ref, inv_ref, g_ref, a1_ref, a2_ref, mean_ref, scale_ref, out_ref, *scratch):
+        *work_refs, v2_ref, z_ref, maps_ref, base_ref, sem = scratch
+        copy = pltpu.make_async_copy(base_in, base_ref, sem)
+        copy.start()
         x = reorder(other_ref[...] - CENTRE, order_ref)
         put(v2_ref, jnp.concatenate([x, x]))
+        copy.wait()
         side_partner(v2_ref, z_ref, base_ref[0, 0, 1])
         pair_maps(lambda j, k, d: z_ref[j + d, k], (g_ref, a1_ref, a2_ref, mean_ref, scale_ref), inv_ref, work_refs, maps_ref)
         finish(maps_ref, order_ref, out_ref)
 
-    def forward(base_ref, other_ref, order_ref, inv_ref, g_ref, a1_ref, a2_ref, mean_ref, scale_ref, out_ref, *scratch):
-        *work_refs, v_ref, y_ref, maps_ref = scratch
+    def forward(base_in, other_ref, order_ref, inv_ref, g_ref, a1_ref, a2_ref, mean_ref, scale_ref, out_ref, *scratch):
+        *work_refs, v_ref, y_ref, maps_ref, base_ref, sem = scratch
+        copy = pltpu.make_async_copy(base_in, base_ref, sem)
+        copy.start()
         put(v_ref, reorder(other_ref[...] - CENTRE, order_ref))
+        copy.wait()
         forward_partner(v_ref, y_ref, base_ref[0, 0, 0])
         pair_maps(lambda j, k, d: y_ref[k + d, j], (g_ref, a1_ref, a2_ref, mean_ref, scale_ref), inv_ref, work_refs, maps_ref)
         finish(maps_ref, order_ref, out_ref)
@@ -322,6 +328,7 @@
             copy.wait()
 
     maps_shape = vmem(nv, 2 * height + SUBS, LANES)
+    base_scratch = [pltpu.SMEM(offsets.shape, i32), pltpu.SemaphoreType.DMA]
     image_shape = vmem(nv, height + SUBS, LANES)
     two_maps = jax.ShapeDtypeStruct((2, height, width), f32)
     whole = jax.ShapeDtypeStruct((8, height, width), f32)
@@ -333,13 +340,13 @@
     )
     side_image, fwd_image = lax.optimization_barrier((side_image, fwd_image))
     side_maps = call(
-        side, (offsets, side_image, order, inv, *stats), [IN_SMEM] + [IN_VMEM] * 8, two_maps, IN_VMEM,
-        work + [maps_shape, vmem(8 + 3, kk, SUBS, LANES), maps_shape], 2**28, "side",
+        side, (offsets, side_image, order, inv, *stats), [IN_VMEM] * 9, two_maps, IN_VMEM,
+        work + [maps_shape, vmem(8 + 3, kk, SUBS, LANES), maps_shape] + base_scratch, 2**28, "side",
     )
     side_back = shifted(side_maps, "strip", 1)
     fwd_maps = call(
-        forward, (offsets, fwd_image, order, inv, *stats), [IN_SMEM] + [IN_VMEM] * 8, two_maps, IN_VMEM,
-        work + [image_shape, vmem(kk + 3, 8, SUBS, LANES), maps_shape], 2**28, "forward",
+        forward, (offsets, fwd_image, order, inv, *stats), [IN_VMEM] * 9, two_maps, IN_VMEM,
+        work + [image_shape, vmem(kk + 3, 8, SUBS, LANES), maps_shape] + base_scratch, 2**28, "forward",
     )
     fwd_back = shifted(fwd_maps, "along", 1)
     out = call(

time: 34 us -> 33.5 us (0.985)
  Pallas kernels: 16.7 us -> 16.2 us
    pallas_call x5, Pallas kernels: 16.7 us -> 16.2 us  [call(): pl.pallas_call(body, in_specs=in_specs, out_specs=out_specs, out_shape=ou...]
where the time goes in v4:
time: 33.5 us; the launch traced here: 32.9 us
  Pallas kernels  16.2 us (48%)
  starting transfers between devices  10.8 us (32%)
  waiting for transfers between devices  4.34 us (13%)
  local copies, waits for them, and re-layouts  1.55 us (5%)
    pallas_call x5, Pallas kernels, call(): pl.pallas_call(body, in_specs=in_specs, out_specs=out_specs, out_shape=ou...  16.2 us
    ppermute x4, starting transfers between devices, shifted(): lax.ppermute(value, axis, [(i, i + steps) for i in range(max(0, -steps),...  10.8 us
    ppermute x4, waiting for transfers between devices, shifted(): lax.ppermute(value, axis, [(i, i + steps) for i in range(max(0, -steps),...  4.34 us
    unnamed x4, local copies, waits for them, and re-layouts  1.55 us
  transfers between devices with their start and end apart: 4, of which 3 were waited for; matrix products, arithmetic and copies ran while one was open for 0% of the time, Pallas kernels for 28%

profile of v4, /device:TPU:1, one launch (start us, length us, event | category | flops | bytes accessed | tf_op | source)
XLA Modules:
  0.0 32.9 jit_solution(15554253044490595365)
XLA Ops:
  0.0 1.3 %collective-permute-start = (f32[64,512]{1,0:T(8,128)}, f32[64,512]{1,0:T(8,128)S(1)}, u32[]{:S(2)}, u32[]{:S(2)}) collective-permute-start(f32[64,512]{1,0:T(8,128)} %image_ref.1), channel_id=1, source_target_pairs={{8,0},{16,8},{24,16},{9,1},{17,9},{25,17},{10,2},{18,10},{26,18},{... | collective-permute-start | bytes 393224 | tf_op jit(solution)/shard_map/ppermute | solution.py:288
  1.3 2.0 %collective-permute-start.1 = (f32[64,512]{1,0:T(8,128)}, f32[64,512]{1,0:T(8,128)S(1)}, u32[]{:S(2)}, u32[]{:S(2)}) collective-permute-start(f32[64,512]{1,0:T(8,128)} %image_ref.1), channel_id=1, source_target_pairs={{1,0},{2,1},{3,2},{4,3},{5,4},{6,5},{7,6},{9,8},{10,9},{11,10},{12... | collective-permute-start | bytes 393224 | tf_op jit(solution)/shard_map/ppermute | solution.py:288
  3.3 0.0 copy-start
  3.3 0.6 %copy-done = s32[1,1,2]{2,1,0:T(1,128)S(1)} copy-done((s32[1,1,2]{2,1,0:T(1,128)S(1)}, s32[1,1,2]{2,1,0:T(1,128)}, u32[]{:S(2)}) %copy-start) | copy-done | bytes 32
  3.9 0.0 copy-start.1
  3.9 0.9 %copy-done.1 = f32[64,512]{1,0:T(8,128)S(1)} copy-done((f32[64,512]{1,0:T(8,128)S(1)}, f32[64,512]{1,0:T(8,128)}, u32[]{:S(2)}) %copy-start.1) | copy-done | bytes 131096
  4.8 1.9 %prepare.1 = (bf16[512,512]{1,0:T(8,128)(2,1)S(1)}, f32[8,16,8,128]{3,2,1,0:T(8,128)S(1)}, f32[8,16,8,128]{3,2,1,0:T(8,128)S(1)}, f32[8,16,8,128]{3,2,1,0:T(8,12...) custom-call(s32[1,1,2]{2,1,0:T(1,128)S(1)} %copy-done, ...), custom_call_target="tpu_custom_call" | custom-call | flops 67108864 | bytes 1048576 | tf_op jit(solution)/shard_map/prepare/pallas_call | solution.py:269
  6.8 0.6 %collective-permute-done.other_ref = f32[64,512]{1,0:T(8,128)S(1)} collective-permute-done((f32[64,512]{1,0:T(8,128)}, f32[64,512]{1,0:T(8,128)S(1)}, u32[]{:S(2)}, u32[]{:S(2)}) %collective-permute-start) | collective-permute-done | bytes 131104 | tf_op jit(solution)/shard_map/ppermute | solution.py:288
  7.4 1.4 %collective-permute-done.1.other_ref = f32[64,512]{1,0:T(8,128)S(1)} collective-permute-done((f32[64,512]{1,0:T(8,128)}, f32[64,512]{1,0:T(8,128)S(1)}, u32[]{:S(2)}, u32[]{:S(2)}) %collective-permute-start.1) | collective-permute-done | bytes 131104 | tf_op jit(solution)/shard_map/ppermute | solution.py:288
  8.7 6.4 %side.1.refs_1_ = f32[2,64,512]{2,1,0:T(8,128)S(1)} custom-call(s32[1,1,2]{2,1,0:T(1,128)S(1)} %copy-done, f32[64,512]{1,0:T(8,128)S(1)} %collective-permute-done.other_ref, bf16[512,512]{1,0:T(8,128)(2,1)S(1)} %get-tuple-element.15.order_ref, f32[8,16,8,128]{3,2,1,0:T(8,128)S(1)} %get-tuple-element.16.inv_ref, ...), custom_call_target="tpu_custom_call" | custom-call | flops 268435456 | bytes 1048576 | tf_op jit(solution)/shard_map/side/pallas_call | solution.py:269
  15.2 4.3 %collective-permute-start.3 = (f32[2,64,512]{2,1,0:T(8,128)S(1)}, f32[2,64,512]{2,1,0:T(8,128)S(1)}, u32[]{:S(2)}, u32[]{:S(2)}) collective-permute-start(f32[2,64,512]{2,1,0:T(8,128)S(1)} %side.1.refs_1_), channel_id=1, source_target_pairs={{0,8},{8,16},{16,24},{1,9},{9,17},{17,25},{2,10},{10,18},{18,26},{... | collective-permute-start | bytes 786440 | tf_op jit(solution)/shard_map/ppermute | solution.py:288
  19.5 6.2 %forward.1.refs_0_ = f32[2,64,512]{2,1,0:T(8,128)S(1)} custom-call(s32[1,1,2]{2,1,0:T(1,128)S(1)} %copy-done, f32[64,512]{1,0:T(8,128)S(1)} %collective-permute-done.1.other_ref, bf16[512,512]{1,0:T(8,128)(2,1)S(1)} %get-tuple-element.15.order_ref, f32[8,16,8,128]{3,2,1,0:T(8,128)S(1)} %get-tuple-element.16.inv_ref, ...), custom_call_target="tpu_custom_call" | custom-call | flops 268435456 | bytes 1048576 | tf_op jit(solution)/shard_map/forward/pallas_call | solution.py:269
  25.7 3.2 %collective-permute-start.2 = (f32[2,64,512]{2,1,0:T(8,128)S(1)}, f32[2,64,512]{2,1,0:T(8,128)S(1)}, u32[]{:S(2)}, u32[]{:S(2)}) collective-permute-start(f32[2,64,512]{2,1,0:T(8,128)S(1)} %forward.1.refs_0_), channel_id=1, source_target_pairs={{0,1},{1,2},{2,3},{3,4},{4,5},{5,6},{6,7},{8,9},{9,10},{10,11},{11... | collective-permute-start | bytes 786440 | tf_op jit(solution)/shard_map/ppermute | solution.py:288
  28.9 0.0 collective-permute-done.3.refs_2_
  28.9 0.9 %collect.1.refs_1_ = f32[8,64,512]{2,1,0:T(8,128)} custom-call(f32[2,64,512]{2,1,0:T(8,128)S(1)} %forward.1.refs_0_, f32[2,64,512]{2,1,0:T(8,128)S(1)} %side.1.refs_1_, f32[2,64,512]{2,1,0:T(8,128)S(1)} %collective-permute-done.3.refs_2_), custom_call_target="tpu_custom_call" | custom-call | flops 1048576 | bytes 1048576 | tf_op jit(solution)/shard_map/collect/pallas_call | solution.py:269
  29.8 2.4 %collective-permute-done.2.refs_0_ = f32[2,64,512]{2,1,0:T(8,128)S(1)} collective-permute-done((f32[2,64,512]{2,1,0:T(8,128)S(1)}, f32[2,64,512]{2,1,0:T(8,128)S(1)}, u32[]{:S(2)}, u32[]{:S(2)}) %collective-permute-start.2) | collective-permute-done | bytes 262176 | tf_op jit(solution)/shard_map/ppermute | solution.py:288
  32.2 0.7 %complete.1 = f32[8,64,512]{2,1,0:T(8,128)} custom-call(f32[2,64,512]{2,1,0:T(8,128)S(1)} %collective-permute-done.2.refs_0_, f32[8,64,512]{2,1,0:T(8,128)} %collect.1.refs_1_), custom_call_target="tpu_custom_call", output_to_operand_aliasing={{}: (1, {})} | custom-call | flops 1048576 | bytes 1048576 | tf_op jit(solution)/shard_map/complete/pallas_call | solution.py:269
Async XLA Ops:
  0.0 7.4 %collective-permute-start = (f32[64,512]{1,0:T(8,128)}, f32[64,512]{1,0:T(8,128)S(1)}, u32[]{:S(2)}, u32[]{:S(2)}) collective-permute-start(f32[64,512]{1,0:T(8,128)} %image_ref.1), channel_id=1, source_target_pairs={{8,0},{16,8},{24,16},{9,1},{17,9},{25,17},{10,2},{18,10},{26,18},{... | collective-permute-start | bytes 393224 | tf_op jit(solution)/shard_map/ppermute | solution.py:288
  1.3 7.4 %collective-permute-start.1 = (f32[64,512]{1,0:T(8,128)}, f32[64,512]{1,0:T(8,128)S(1)}, u32[]{:S(2)}, u32[]{:S(2)}) collective-permute-start(f32[64,512]{1,0:T(8,128)} %image_ref.1), channel_id=1, source_target_pairs={{1,0},{2,1},{3,2},{4,3},{5,4},{6,5},{7,6},{9,8},{10,9},{11,10},{12... | collective-permute-start | bytes 393224 | tf_op jit(solution)/shard_map/ppermute | solution.py:288
  3.3 0.7 %copy-start = (s32[1,1,2]{2,1,0:T(1,128)S(1)}, s32[1,1,2]{2,1,0:T(1,128)}, u32[]{:S(2)}) copy-start(s32[1,1,2]{2,1,0:T(1,128)} %base_in.3) | copy-start | bytes 28
  3.9 0.9 %copy-start.1 = (f32[64,512]{1,0:T(8,128)S(1)}, f32[64,512]{1,0:T(8,128)}, u32[]{:S(2)}) copy-start(f32[64,512]{1,0:T(8,128)} %image_ref.1) | copy-start | bytes 393220
  15.2 13.8 %collective-permute-start.3 = (f32[2,64,512]{2,1,0:T(8,128)S(1)}, f32[2,64,512]{2,1,0:T(8,128)S(1)}, u32[]{:S(2)}, u32[]{:S(2)}) collective-permute-start(f32[2,64,512]{2,1,0:T(8,128)S(1)} %side.1.refs_1_), channel_id=1, source_target_pairs={{0,8},{8,16},{16,24},{1,9},{9,17},{17,25},{2,10},{10,18},{18,26},{... | collective-permute-start | bytes 786440 | tf_op jit(solution)/shard_map/ppermute | solution.py:288
  25.7 6.5 %collective-permute-start.2 = (f32[2,64,512]{2,1,0:T(8,128)S(1)}, f32[2,64,512]{2,1,0:T(8,128)S(1)}, u32[]{:S(2)}, u32[]{:S(2)}) collective-permute-start(f32[2,64,512]{2,1,0:T(8,128)S(1)} %forward.1.refs_0_), channel_id=1, source_target_pairs={{0,1},{1,2},{2,3},{3,4},{4,5},{5,6},{6,7},{8,9},{9,10},{10,11},{11... | collective-permute-start | bytes 786440 | tf_op jit(solution)/shard_map/ppermute | solution.py:288
